TPU v7x, 32 devices: a whole 2x2x4 slice. The times are simulated.
32 devices in a mesh: grp: 2 (over y), row: 8 (over z, x), col: 2 (over core).
Axes of the slice: x: 2, y: 2, z: 4, core: 2. Of those that a mesh axis runs over, the one named last changes fastest.
Arguments:
- tokens: bfloat16 [128, 256, 180], P(('grp', 'row'), 'col'), parts along dimension 0, may hold values from -6 to 6
- grad_out: bfloat16 [128, 256, 180], P(('grp', 'row'), 'col'), parts along dimension 0, may hold values from -8 to 8
- regions: int32 [128, 256], P(('grp', 'row'), 'col'), parts along dimension 0, may hold values from 0 to 15, as said below
- ln_gain: float32 [180], replicated, may hold values from 0.1 to 1.9
- ln_offset: float32 [180], replicated, may hold values from -1.5 to 1.5
- qkv_weight: bfloat16 [180, 540], replicated, may hold values from -0.4375 to 0.4375
- qkv_bias: float32 [540], replicated, may hold values from -1.5 to 1.5
- proj_weight: bfloat16 [180, 180], replicated, may hold values from -0.4375 to 0.4375
- bias_table: float32 [225, 6], replicated, may hold values from -4 to 320
Outputs:
- d_tokens: bfloat16 [128, 256, 180], P(('grp', 'row'), 'col'), parts along dimension 0
- d_qkv_weight: float32 [360, 540], P('grp'), parts along dimension 0
- d_qkv_bias: float32 [1080], P('grp'), parts along dimension 0
- d_proj_weight: float32 [360, 180], P('grp'), parts along dimension 0
- d_bias_table: float32 [450, 6], P('grp'), parts along dimension 0
- d_ln_gain: float32 [360], P('grp'), parts along dimension 0
- d_ln_offset: float32 [360], P('grp'), parts along dimension 0
There are 2 independent parts, one for each index of `grp`. A program takes and returns all parts, laid end to end along the dimension named above; an argument that names none is the same for every part. Nothing has to cross between parts.
Inputs may be any that keep to these rules, and one draw needn't show every extreme that they name: `regions`: A token attends only to tokens of its window with the same id. The map is a grid: the id is 4 a + b, where a, from 0 to 3, depends only on the token's row and b, from 0 to 3, only on its column.
All inputs are finite; a program needn't handle non-finite values.
Results may differ from a plain program's by a relative error of at most 0.0085.
Values may be sent and summed in bfloat16 or wider, within the bound.
A program may use at most 64 MiB of HBM per device.

v0:
```python
import functools

import jax
import jax.numpy as jnp
from jax import lax
from jax.experimental import pallas as pl
from jax.experimental.pallas import tpu as pltpu
from jax.sharding import PartitionSpec as P

HEADS = 6
WIN = 8
SHIFT = 4
SPAN = WIN * WIN
C = 180
HEAD = C // HEADS
LANES = HEADS * SPAN
BLOCK = 184
EDGE = 16
MASKED = -10000.0
MESH = pl.DeviceIdType.MESH
F32 = jnp.float32
BF16 = jnp.bfloat16

NN = (((1,), (0,)), ((), ()))
NT = (((1,), (1,)), ((), ()))
TN = (((0,), (0,)), ((), ()))


def mul(left, right, form=NN):
    return lax.dot_general(left, right, form, preferred_element_type=F32)


def exact(left, right, form=NN):
    return lax.dot_general(
        left, right, form, preferred_element_type=F32, precision=lax.Precision.HIGHEST
    )


def split_mul(left, picks):
    high = left.astype(BF16)
    low = (left - high.astype(F32)).astype(BF16)
    return mul(high, picks) + mul(low, picks)


def iota(shape, dim):
    return lax.broadcasted_iota(jnp.int32, shape, dim)


def col_spread(cj):
    src = iota((SPAN, 128), 0)
    dst = iota((SPAN, 128), 1)
    return (dst == (src >> 3) * 16 + (src & 7) - cj + 7).astype(F32)


def row_spread(rj):
    src = iota((128, 256), 0)
    dst = iota((128, 256), 1)
    return (dst == src + 16 * (7 - rj)).astype(F32)


def table_spread(entries):
    src = iota((entries, 256), 0)
    dst = iota((entries, 256), 1)
    hit = (src == (dst >> 4) * 15 + (dst & 15)) & ((dst & 15) < 15) & (dst < 240)
    return hit.astype(F32)


def body(
    rows_n, cols_n, rows_total, out_scale,
    both, reg, gain_ref, offset_ref, qkvw, qkvb, projw, table,
    d_tok, d_qkvw, d_qkvb, d_projw, d_table, d_gain, d_offset,
    both_b, both_r, both_d, reg_b, reg_r,
    unit, inv_std, gradf, nt_s, q_s, k_s, v_s, da_s, gb_s, att, dq_s, dk_s, dv_s,
    w_s, b_s, bias_t, span_a, span_b, hmask, lab_col, lab_row, score_acc,
    fold_a, fold_b, frame_low, frame_two, back_u, back_l, back_ul,
    pack, pack_low, pair_in, half_low, part_in, result,
    halo_send, halo_recv, back_send, back_recv, pair_sem,
    part_send, part_recv, all_send, all_recv, fwd_send, fwd_recv,
):
    row = lax.axis_index("row")
    col = lax.axis_index("col")
    up = lax.rem(row + rows_n - 1, rows_n)
    down = lax.rem(row + 1, rows_n)
    other = lax.rem(col + 1, cols_n)
    tile_cols = both.shape[1]
    wins = tile_cols // WIN
    count = wins * SPAN
    half = rows_total // 2
    chunk = half // rows_n

    def remote(src, dst, send, recv, to_row, to_col):
        return pltpu.make_async_remote_copy(
            src_ref=src, dst_ref=dst, send_sem=send, recv_sem=recv,
            device_id={"row": to_row, "col": to_col}, device_id_type=MESH,
        )

    barrier = pltpu.get_barrier_semaphore()

    @pl.loop(1, rows_n)
    def _(k):
        pl.semaphore_signal(
            barrier, inc=1, device_id={"row": lax.rem(row + k, rows_n), "col": col},
            device_id_type=MESH,
        )

    for to_row in (row, up, down):
        pl.semaphore_signal(
            barrier, inc=1, device_id={"row": to_row, "col": other}, device_id_type=MESH
        )
    pl.semaphore_wait(barrier, rows_n + 2)

    step_wins = 4
    step = step_wins * SPAN
    steps = wins // step_wins
    span_cols = step_wins * WIN

    def halo(i, src, dst, to_row, to_col):
        return remote(src, dst, halo_send.at[i], halo_recv.at[i], to_row, to_col)

    labels = [halo(0, reg, reg_b, up, col), halo(1, reg, reg_r, row, other)]
    sides = [
        halo(2, both.at[SHIFT:WIN, 0:EDGE], both_r, row, other),
        halo(3, both.at[0:SHIFT, 0:EDGE], both_d, up, other),
    ]
    chunks = []
    for b in range(steps):
        first = b * span_cols + (EDGE if b else 0)
        last = min((b + 1) * span_cols + EDGE, tile_cols)
        src, dst = both.at[0:SHIFT, first:last], both_b.at[0:SHIFT, first:last]
        chunks.append([halo(4 + b, src, dst, up, col)])
    for copy in labels + chunks[0] + sides + chunks[1]:
        copy.start()

    flat = exact(table[...], table_spread(table.shape[1]))
    for rj in range(WIN):
        span_b[pl.ds(rj, HEADS, stride=WIN), :] = exact(flat, row_spread(rj), NT)
    for cj in range(WIN):
        span_a[pl.ds(cj, HEADS * WIN, stride=WIN), :] = exact(span_b[...], col_spread(cj), NT)
    for h in range(HEADS):
        bias_t[:, h * SPAN : (h + 1) * SPAN] = span_a[h * SPAN : (h + 1) * SPAN, :]
    mask_row = iota((LANES, C), 0) >> 6
    mask_col = iota((LANES, C), 1)
    hmask[...] = (
        (mask_col >= mask_row * HEAD) & (mask_col < (mask_row + 1) * HEAD)
    ).astype(F32).astype(BF16)
    score_acc[...] = jnp.zeros_like(score_acc)
    pack[...] = jnp.zeros_like(pack)

    nt_s[...] = jnp.ones_like(nt_s)
    for cj in range(WIN):
        fold_a[cj * SPAN : (cj + 1) * SPAN, :] = col_spread(cj).astype(BF16)
    for rj in range(WIN):
        fold_b[rj * 128 : (rj + 1) * 128, :] = row_spread(rj).astype(BF16)
    weights = qkvw[...]
    offsets = qkvb[...]
    for i in range(3):
        w_s[i] = weights[:, i * C : (i + 1) * C]
        b_s[i] = offsets[:, i * C : (i + 1) * C]

    for copy in labels:
        copy.wait()

    own = reg[...]
    row_part = jnp.concatenate([own[SHIFT:], reg_b[0:SHIFT, :]], 0)[:, 0:1] >> 2
    col_own = pltpu.roll(own, tile_cols - SHIFT, 1)
    col_right = pltpu.roll(reg_r[...], tile_cols - SHIFT, 1)
    col_part = jnp.where(iota((WIN, tile_cols), 1) < tile_cols - SHIFT, col_own, col_right)[0:1] & 3
    label = (row_part * 4 + col_part).astype(F32)
    spread = jnp.broadcast_to(label[:, None, :], (WIN, WIN, tile_cols)).reshape(SPAN, tile_cols)
    spread = jnp.where(
        (iota((SPAN, tile_cols), 0) & 7) == (iota((SPAN, tile_cols), 1) & 7), spread, 0.0
    )
    pick = ((iota((tile_cols, wins), 0) >> 3) == iota((tile_cols, wins), 1)).astype(F32)
    columns = exact(spread, pick)
    tiled = (iota((SPAN, LANES), 0) == (iota((SPAN, LANES), 1) & (SPAN - 1))).astype(F32)
    lab_row[...] = exact(columns, tiled, TN)
    for w in range(wins):
        lab_col[w] = jnp.broadcast_to(columns[:, w : w + 1], (SPAN, 128))

    def gather_heads(stacked):
        kept = stacked * hmask[...].astype(F32)
        return jnp.sum(kept.reshape(HEADS, SPAN, C), 0)

    small = 4 * BLOCK
    edge = tile_cols - EDGE
    backs = []

    def back(src, dst, to_row, to_col):
        i = len(backs)
        backs.append(remote(src, dst, back_send.at[i], back_recv.at[i], to_row, to_col))
        backs[-1].start()

    for b in range(steps):
        for copy in chunks[b] + (sides if b == steps - 1 else []):
            copy.wait()
        if b + 2 < steps:
            for copy in chunks[b + 2]:
                copy.start()
        at = slice(b * step, (b + 1) * step)
        win_at = slice(b * step_wins, (b + 1) * step_wins)
        cols = slice(b * span_cols, (b + 1) * span_cols)
        near = slice(b * span_cols, min((b + 1) * span_cols + EDGE, tile_cols))

        for r in range(WIN):
            if r < SHIFT:
                part, beyond = both[r + SHIFT, near], both_r[r]
            else:
                part, beyond = both_b[r - SHIFT, near], both_d[r - SHIFT]
            wide = part.astype(F32)
            if b == steps - 1:
                wide = jnp.concatenate([wide, beyond.astype(F32)], 0)
            wide = wide[SHIFT : SHIFT + span_cols]
            unit[win_at, r] = wide[:, 0:C].reshape(step_wins, WIN, C)
            gradf[win_at, r] = wide[:, C : 2 * C].reshape(step_wins, WIN, C)

        x = unit[win_at].reshape(step, C)
        center = jnp.mean(x, -1, keepdims=True)
        x = x - center
        inv = lax.rsqrt(jnp.mean(x * x, -1, keepdims=True) + 1e-05)
        x = x * inv
        unit[win_at] = x.reshape(step_wins, WIN, WIN, C)
        inv_std[at] = inv
        n = (x * gain_ref[...] + offset_ref[...]).astype(BF16)
        nt_s[0:C, at] = n.T
        q_s[at] = ((mul(n, w_s[0]) + b_s[0]) * HEAD ** (-0.5)).astype(BF16)
        k_s[at] = (mul(n, w_s[1]) + b_s[1]).astype(BF16)
        v_s[at] = (mul(n, w_s[2]) + b_s[2]).astype(BF16)
        g = gradf[win_at].reshape(step, C).astype(BF16)
        gb_s[at] = g
        da_s[at] = mul(g, projw[...], NT).astype(BF16)

        @pl.loop(0, step_wins // 2)
        def _(pair_at):
            loaded = []
            for i in range(2):
                w = b * step_wins + pair_at * 2 + i
                at = pl.ds(pl.multiple_of(w * SPAN, SPAN), SPAN)
                same = lab_col[w][:, 0:1] == lab_row[pl.ds(w, 1), :]
                loaded.append((at, q_s[at], k_s[at], v_s[at], da_s[at], same))
            heads = hmask[...]
            bias = bias_t[...]
            total = score_acc[...]
            for at, q, k, v, da, same in loaded:
                qm = jnp.concatenate([q] * HEADS, 0) * heads
                dam = jnp.concatenate([da] * HEADS, 0) * heads
                scores = jnp.where(same, mul(k, qm, NT) + bias, MASKED)
                e = jnp.exp(scores - jnp.max(scores, 0, keepdims=True))
                p = e * (1.0 / jnp.sum(e, 0, keepdims=True))
                p_low = p.astype(BF16)
                att[at] = gather_heads(mul(p_low, v, TN)).astype(BF16)
                dp = mul(v, dam, NT)
                ds = p * (dp - jnp.sum(p * dp, 0, keepdims=True))
                total += ds
                ds_low = ds.astype(BF16)
                dq_s[at] = (gather_heads(mul(ds_low, k, TN)) * HEAD ** (-0.5)).astype(BF16)
                dk_s[at] = mul(ds_low, qm).astype(BF16)
                dv_s[at] = mul(p_low, dam).astype(BF16)
            score_acc[...] = total

        x = unit[win_at].reshape(step, C)
        dn = mul(dq_s[at], w_s[0], NT) + mul(dk_s[at], w_s[1], NT) + mul(dv_s[at], w_s[2], NT)
        pack[small + 3 : small + 4, 0:C] += jnp.sum(dn * x, 0, keepdims=True)
        pack[small + 4 : small + 5, 0:C] += jnp.sum(dn, 0, keepdims=True)
        g = dn * gain_ref[...]
        dx = inv_std[at] * (
            g - jnp.mean(g, -1, keepdims=True) - x * jnp.mean(g * x, -1, keepdims=True)
        )
        out = (gradf[win_at].reshape(step, C) + dx).reshape(step_wins, WIN, WIN, C)
        for r in range(SHIFT):
            frame_low[r, cols] = out[:, r].reshape(span_cols, C).astype(BF16)
        for r in range(0, SHIFT, 2):
            two = [out[:, SHIFT + r + i].reshape(span_cols, C) for i in range(2)]
            frame_two[r // 2, cols] = jnp.concatenate(two, 1).astype(BF16)
        back(frame_two.at[0:2, cols], back_u.at[0:2, cols], down, col)
        if b == steps - 1:
            back(frame_low.at[0:SHIFT, edge:tile_cols], back_l, row, other)
            back(frame_two.at[0:2, edge:tile_cols], back_ul, down, other)

    for i, part in enumerate((dq_s, dk_s, dv_s)):
        pack[i * BLOCK : (i + 1) * BLOCK, 0:C] = mul(nt_s[...], part[...])[0:BLOCK]
    pack[3 * BLOCK : 3 * BLOCK + C, 0:C] = mul(att[...], gb_s[...], TN)
    for h in range(HEADS):
        span_a[h * SPAN : (h + 1) * SPAN, :] = score_acc[:, h * SPAN : (h + 1) * SPAN]
    wide = jnp.concatenate(
        [span_a[pl.ds(cj, HEADS * WIN, stride=WIN), :] for cj in range(WIN)], 1
    )
    span_b[...] = split_mul(wide, fold_a[...])
    wide = jnp.concatenate(
        [span_b[pl.ds(rj, HEADS, stride=WIN), :] for rj in range(WIN)], 1
    )
    flat_sum = split_mul(wide, fold_b[...])
    pack[small + 8 : small + 8 + HEADS, :] = flat_sum
    pack_low[...] = pack[...].astype(BF16)

    pair = remote(
        pack_low.at[pl.ds(pl.multiple_of(other * half, 16), half)], pair_in,
        pair_sem.at[0], pair_sem.at[1], row, other,
    )
    pair.start()
    pair.wait()
    mine = pl.ds(pl.multiple_of(col * half, 16), half)
    half_low[...] = (pack[mine] + pair_in[...].astype(F32)).astype(BF16)

    def part_copy(k):
        peer = lax.rem(row + k, rows_n)
        return remote(
            half_low.at[pl.ds(pl.multiple_of(peer * chunk, 16), chunk)], part_in.at[k],
            part_send.at[k], part_recv.at[k], peer, col,
        )

    @pl.loop(1, rows_n)
    def _(k):
        part_copy(k).start()

    for copy in backs:
        copy.wait()
    for r in range(WIN):
        if r < SHIFT:
            lanes = slice((r % 2) * C, (r % 2 + 1) * C)
            left_part = back_ul[r // 2].astype(F32)[:, lanes]
            main_part = back_u[r // 2].astype(F32)[:, lanes]
        else:
            left_part, main_part = back_l[r - SHIFT], frame_low[r - SHIFT]
        wide = jnp.concatenate([left_part.astype(F32), main_part.astype(F32)], 0)
        d_tok[r] = wide[EDGE - SHIFT : EDGE - SHIFT + tile_cols].astype(BF16)

    def add_part(k, total):
        part_copy(k).wait()
        return total + part_in[k].astype(F32)

    my_chunk = pl.ds(pl.multiple_of(row * chunk, 16), chunk)
    total = lax.fori_loop(1, rows_n, add_part, half_low[my_chunk].astype(F32))
    own_chunk = result.at[col, my_chunk]
    own_chunk[...] = total.astype(BF16)

    def all_copy(k):
        return remote(
            own_chunk, own_chunk, all_send.at[k], all_recv.at[k],
            lax.rem(row + k, rows_n), col,
        )

    def forward(k):
        source = lax.rem(row + rows_n - k, rows_n)
        piece = result.at[col, pl.ds(pl.multiple_of(source * chunk, 16), chunk)]
        return remote(piece, piece, fwd_send.at[k], fwd_recv.at[k], row, other)

    @pl.loop(1, rows_n)
    def _(k):
        all_copy(k).start()

    forward(0).start()

    @pl.loop(1, rows_n)
    def _(k):
        all_copy(k).wait()
        forward(k).start()

    @pl.loop(0, rows_n)
    def _(k):
        forward(k).wait()

    pack[0:half] = result[0].astype(F32) * out_scale
    pack[half : 2 * half] = result[1].astype(F32) * out_scale
    d_qkvw[...] = jnp.concatenate(
        [pack[i * BLOCK : i * BLOCK + C, 0:C] for i in range(3)], 1
    )
    d_qkvb[...] = jnp.concatenate(
        [pack[i * BLOCK + C : i * BLOCK + C + 1, 0:C] for i in range(3)], 1
    )
    d_projw[...] = pack[3 * BLOCK : 3 * BLOCK + C, 0:C]
    d_gain[...] = pack[small + 3 : small + 4, 0:C]
    d_offset[...] = pack[small + 4 : small + 5, 0:C]
    entries = table_spread(d_table.shape[1])
    d_table[...] = exact(pack[small + 8 : small + 8 + HEADS, :], entries, NT)


def on_device(
    tokens, grad_out, regions, ln_gain, ln_offset, qkv_weight, qkv_bias, proj_weight, bias_table
):
    rows_n, cols_n = lax.axis_size("row"), lax.axis_size("col")
    tile_cols = tokens.shape[1]
    wins = tile_cols // WIN
    count = wins * SPAN
    steps = wins // 4
    unit_rows = 2 * 16 * rows_n
    needed = 4 * BLOCK + 16
    rows_total = -(-needed // unit_rows) * unit_rows
    half = rows_total // 2
    chunk = half // rows_n
    total_tokens = tokens.shape[0] * tile_cols * rows_n * cols_n
    vmem = pltpu.VMEM
    halo = [
        vmem((SHIFT, tile_cols, 2 * C), BF16),
        vmem((SHIFT, EDGE, 2 * C), BF16),
        vmem((SHIFT, EDGE, 2 * C), BF16),
    ]
    home = [
        vmem((SHIFT, tile_cols, C), BF16),
        vmem((2, tile_cols, 2 * C), BF16),
        vmem((2, tile_cols, 2 * C), BF16),
        vmem((SHIFT, EDGE, C), BF16),
        vmem((2, EDGE, 2 * C), BF16),
    ]
    flat_low = vmem((count, C), BF16)
    whole = pl.BlockSpec(memory_space=pltpu.VMEM)
    dma = pltpu.SemaphoreType.DMA
    outs = pl.pallas_call(
        functools.partial(body, rows_n, cols_n, rows_total, total_tokens ** (-0.5)),
        out_shape=(
            jax.ShapeDtypeStruct(tokens.shape, BF16),
            jax.ShapeDtypeStruct((C, 3 * C), F32),
            jax.ShapeDtypeStruct((1, 3 * C), F32),
            jax.ShapeDtypeStruct((C, C), F32),
            jax.ShapeDtypeStruct((HEADS, bias_table.shape[0]), F32),
            jax.ShapeDtypeStruct((1, C), F32),
            jax.ShapeDtypeStruct((1, C), F32),
        ),
        in_specs=[whole] * 8,
        out_specs=(whole,) * 7,
        scratch_shapes=halo + [
            vmem(regions.shape, jnp.int32),
            vmem(regions.shape, jnp.int32),
            vmem((wins, WIN, WIN, C), F32),
            vmem((count, 1), F32),
            vmem((wins, WIN, WIN, C), F32),
            vmem((192, count), BF16),
        ] + [flat_low] * 9 + [
            vmem((3, C, C), BF16),
            vmem((3, 1, C), F32),
            vmem((SPAN, LANES), F32),
            vmem((HEADS * SPAN, SPAN), F32),
            vmem((HEADS * WIN, 128), F32),
            vmem((LANES, C), BF16),
            vmem((wins, SPAN, 128), F32),
            vmem((wins, LANES), F32),
            vmem((SPAN, LANES), F32),
            vmem((WIN * SPAN, 128), BF16),
            vmem((WIN * 128, 256), BF16),
        ] + home + [
            vmem((rows_total, 256), F32),
            vmem((rows_total, 256), BF16),
            vmem((half, 256), BF16),
            vmem((half, 256), BF16),
            vmem((rows_n, chunk, 256), BF16),
            vmem((2, half, 256), BF16),
            dma((4 + steps,)), dma((4 + steps,)),
            dma((steps + 2,)), dma((steps + 2,)), dma((2,)),
            dma((rows_n,)), dma((rows_n,)), dma((rows_n,)), dma((rows_n,)),
            dma((rows_n,)), dma((rows_n,)),
        ],
        compiler_params=pltpu.CompilerParams(
            collective_id=0, has_side_effects=True, vmem_limit_bytes=48 * 1024 * 1024
        ),
    )(
        jnp.concatenate([tokens, grad_out], -1), regions, ln_gain.reshape(1, C), ln_offset.reshape(1, C), qkv_weight,
        qkv_bias.reshape(1, 3 * C), proj_weight, bias_table.T,
    )
    d_tokens, d_qkvw, d_qkvb, d_projw, d_table, d_gain, d_offset = outs
    return (
        d_tokens,
        d_qkvw,
        d_qkvb.reshape(3 * C),
        d_projw,
        d_table.T,
        d_gain.reshape(C),
        d_offset.reshape(C),
    )


def solution(mesh):
    placed = (
        P(("grp", "row"), "col", None),
        P(("grp", "row"), "col", None),
        P(("grp", "row"), "col"),
        P(),
        P(),
        P(),
        P(),
        P(),
        P(),
    )
    return jax.shard_map(
        on_device,
        mesh=mesh,
        in_specs=placed,
        out_specs=(
            P(("grp", "row"), "col", None),
            P("grp", None),
            P("grp"),
            P("grp", None),
            P("grp", None),
            P("grp"),
            P("grp"),
        ),
        check_vma=False,
    )
```

profile of v0, /device:TPU:0, one launch (start us, length us, event | category | flops | bytes accessed | tf_op | source)
XLA Modules:
  0.0 52.2 jit_solution(10294121952461330066)
XLA Ops:
  0.6 0.0 copy-start.6
  0.6 0.7 %reshape.34.qkvb = f32[1,540]{1,0:T(1,128)S(1)} reshape(f32[540]{0:T(1024)} %param.15) | data formatting | bytes 4320 | tf_op jit(solution)/shard_map/reshape | solution.py:456
  1.4 1.2 %copy.16 = bf16[8,128,180]{2,1,0:T(8,128)(2,1)S(1)} copy(bf16[8,128,180]{1,0,2:T(8,128)(2,1)} %param.9) | data formatting | bytes 737280 | tf_op args[0]
  2.6 0.0 copy-done.6
  2.6 0.3 copy.17
  2.9 0.0 copy-start
  3.0 0.0 copy-start.1
  3.0 0.0 copy-start.2
  3.0 0.0 copy-start.3
  3.0 0.0 copy-start.4
  3.0 0.0 copy-start.5
  3.0 0.3 pad_maximum_fusion.both
  3.3 0.6 %copy-done = bf16[180,540]{1,0:T(8,128)(2,1)S(1)} copy-done((bf16[180,540]{1,0:T(8,128)(2,1)S(1)}, bf16[180,540]{1,0:T(8,128)(2,1)}, u32[]{:S(2)}) %copy-start) | copy-done | bytes 194424
  3.9 0.1 copy-done.1
  4.0 0.0 copy-done.2
  4.0 0.0 copy-done.3
  4.0 0.0 copy-done.4
  4.0 0.0 copy-done.5
  4.0 43.5 %shard_map.144 = (bf16[8,128,180]{2,1,0:T(8,128)(2,1)S(1)}, f32[180,540]{1,0:T(8,128)S(1)}, f32[1,540]{1,0:T(1,128)S(1)}, f32[180,180]{1,0:T(8,128)S(1)}, f32[6,...) custom-call(bf16[8,128,360]{2,1,0:T(8,128)(2,1)S(1)} %pad_maximum_fusion.both, s32[8,128]{1,0:T(8,128)S(1)} %copy-done.3, ...), custom_call_target="tpu_custom_call" | custom-call | tf_op jit(solution)/shard_map/pallas_call | solution.py:407
  47.4 1.0 %copy.18 = bf16[8,128,180]{1,0,2:T(8,128)(2,1)} copy(bf16[8,128,180]{2,1,0:T(8,128)(2,1)S(1)} %get-tuple-element.21) | data formatting | bytes 737280
  48.4 0.6 %reduce = f32[540]{0:T(1024)} reduce(f32[1,540]{1,0:T(1,128)S(1)} %get-tuple-element.16, f32[]{:T(128)} %constant.3), dimensions={0}, to_apply=%get-tuple-element.16.reduce_sub_computation | reduce | bytes 4324 | tf_op jit(solution)/shard_map/pallas_call | solution.py:407
  49.0 0.8 %copy.24 = f32[180,540]{1,0:T(8,128)} copy(f32[180,540]{1,0:T(8,128)S(1)} %get-tuple-element.36) | data formatting | bytes 777600
  49.8 0.7 %copy.25 = f32[180,180]{1,0:T(8,128)} copy(f32[180,180]{1,0:T(8,128)S(1)} %get-tuple-element.38) | data formatting | bytes 259200
  50.5 0.6 %copy.26 = f32[225,6]{0,1:T(8,128)} copy(f32[225,6]{0,1:T(8,128)S(1)} %bitcast.7) | data formatting | bytes 10800
  51.1 0.6 %copy.27 = f32[180]{0:T(256)} copy(f32[180]{0:T(256)S(1)} %bitcast.9) | data formatting | bytes 1440
  51.7 0.6 %copy.28 = f32[180]{0:T(256)} copy(f32[180]{0:T(256)S(1)} %bitcast.8) | data formatting | bytes 1440
Async XLA Ops:
  0.6 2.0 %copy-start.6 = (bf16[8,128,180]{1,0,2:T(8,128)(2,1)S(1)}, bf16[8,128,180]{1,0,2:T(8,128)(2,1)}, u32[]{:S(2)}) copy-start(bf16[8,128,180]{1,0,2:T(8,128)(2,1)} %param.10) | copy-start | bytes 1105924
  2.9 0.9 %copy-start = (bf16[180,540]{1,0:T(8,128)(2,1)S(1)}, bf16[180,540]{1,0:T(8,128)(2,1)}, u32[]{:S(2)}) copy-start(bf16[180,540]{1,0:T(8,128)(2,1)} %qkvw.1) | copy-start | bytes 583204
  3.0 1.0 %copy-start.1 = (bf16[180,180]{1,0:T(8,128)(2,1)S(1)}, bf16[180,180]{1,0:T(8,128)(2,1)}, u32[]{:S(2)}) copy-start(bf16[180,180]{1,0:T(8,128)(2,1)} %projw.1) | copy-start | bytes 194404
  3.0 1.0 %copy-start.2 = (f32[225,6]{0,1:T(8,128)S(1)}, f32[225,6]{0,1:T(8,128)}, u32[]{:S(2)}) copy-start(f32[225,6]{0,1:T(8,128)} %param.17) | copy-start | bytes 16204
  3.0 1.0 %copy-start.3 = (s32[8,128]{1,0:T(8,128)S(1)}, s32[8,128]{1,0:T(8,128)}, u32[]{:S(2)}) copy-start(s32[8,128]{1,0:T(8,128)} %reg.1) | copy-start | bytes 12292
  3.0 1.0 %copy-start.4 = (f32[180]{0:T(256)S(1)}, f32[180]{0:T(256)}, u32[]{:S(2)}) copy-start(f32[180]{0:T(256)} %param.12) | copy-start | bytes 2164
  3.0 1.0 %copy-start.5 = (f32[180]{0:T(256)S(1)}, f32[180]{0:T(256)}, u32[]{:S(2)}) copy-start(f32[180]{0:T(256)} %param.13) | copy-start | bytes 2164
where the time goes:
time: 52.4 us; the launch traced here: 52.2 us
  Pallas kernels  43.5 us (83%)
  local copies, waits for them, and re-layouts  7.11 us (14%)
  other arithmetic  0.91 us (2%)
  between operations  0.73 us (1%)
    pallas_call x1, Pallas kernels, on_device(): pl.pallas_call(functools.partial(body, rows_n, cols_n, rows_total, total_...  43.5 us
    unnamed x22, local copies, waits for them, and re-layouts  6.38 us

commit v1 on v0

--- a/solution.py
+++ b/solution.py
@@ -14,7 +14,10 @@
 C = 180
 HEAD = C // HEADS
 LANES = HEADS * SPAN
-BLOCK = 184
+BLOCK = 192
+LANE = 128
+WIDE = 2 * LANE
+HEADW = 32
 EDGE = 16
 MASKED = -10000.0
 MESH = pl.DeviceIdType.MESH
@@ -63,6 +66,26 @@
     dst = iota((entries, 256), 1)
     hit = (src == (dst >> 4) * 15 + (dst & 15)) & ((dst & 15) < 15) & (dst < 240)
     return hit.astype(F32)
+
+
+def head_spread():
+    src = iota((C, WIDE), 0)
+    lane = iota((1, WIDE), 1)
+    head, place = lane >> 5, lane & (HEADW - 1)
+    wanted = jnp.where((place < HEAD) & (head < HEADS), head * HEAD + place, -1)
+    return (src == wanted).astype(F32).astype(BF16)
+
+
+def part_pick():
+    lane = iota((1, 3 * C), 1)
+    part = (lane >= C).astype(jnp.int32) + (lane >= 2 * C).astype(jnp.int32)
+    place = lane - part * C
+    head = sum((place >= t * HEAD).astype(jnp.int32) for t in range(1, HEADS))
+    place = place - head * HEAD
+    near = part * LANE + head * HEADW + place
+    far = 3 * LANE + (part >> 1) * LANE + (part & 1) * 64 + (head - 4) * HEADW + place
+    wanted = jnp.where(head < 4, near, far)
+    return (iota((5 * LANE, 3 * C), 0) == wanted).astype(F32).astype(BF16)
 
 
 def body(
@@ -71,7 +94,7 @@
     d_tok, d_qkvw, d_qkvb, d_projw, d_table, d_gain, d_offset,
     both_b, both_r, both_d, reg_b, reg_r,
     unit, inv_std, gradf, nt_s, q_s, k_s, v_s, da_s, gb_s, att, dq_s, dk_s, dv_s,
-    w_s, b_s, bias_t, span_a, span_b, hmask, lab_col, lab_row, score_acc,
+    w_s, b_s, pw_s, e_s, pick_s, bias_t, span_a, span_b, hmask, lab_col, lab_row, score_acc, sums,
     fold_a, fold_b, frame_low, frame_two, back_u, back_l, back_ul,
     pack, pack_low, pair_in, half_low, part_in, result,
     halo_send, halo_recv, back_send, back_recv, pair_sem,
@@ -128,6 +151,7 @@
         last = min((b + 1) * span_cols + EDGE, tile_cols)
         src, dst = both.at[0:SHIFT, first:last], both_b.at[0:SHIFT, first:last]
         chunks.append([halo(4 + b, src, dst, up, col)])
+    small = 6 * BLOCK
     for copy in labels + chunks[0] + sides + chunks[1]:
         copy.start()
 
@@ -138,13 +162,13 @@
         span_a[pl.ds(cj, HEADS * WIN, stride=WIN), :] = exact(span_b[...], col_spread(cj), NT)
     for h in range(HEADS):
         bias_t[:, h * SPAN : (h + 1) * SPAN] = span_a[h * SPAN : (h + 1) * SPAN, :]
-    mask_row = iota((LANES, C), 0) >> 6
-    mask_col = iota((LANES, C), 1)
-    hmask[...] = (
-        (mask_col >= mask_row * HEAD) & (mask_col < (mask_row + 1) * HEAD)
-    ).astype(F32).astype(BF16)
+    mask_row = iota((4 * 16, LANE), 0) >> 4
+    hmask[...] = ((iota((4 * 16, LANE), 1) >> 5) == mask_row).astype(F32).astype(BF16)
+    e_s[...] = head_spread()
+    pick_s[...] = part_pick()
     score_acc[...] = jnp.zeros_like(score_acc)
-    pack[...] = jnp.zeros_like(pack)
+    sums[...] = jnp.zeros_like(sums)
+    pack[small:] = jnp.zeros_like(pack[small:])
 
     nt_s[...] = jnp.ones_like(nt_s)
     for cj in range(WIN):
@@ -154,8 +178,9 @@
     weights = qkvw[...]
     offsets = qkvb[...]
     for i in range(3):
-        w_s[i] = weights[:, i * C : (i + 1) * C]
-        b_s[i] = offsets[:, i * C : (i + 1) * C]
+        w_s[i] = mul(weights[:, i * C : (i + 1) * C], e_s[...]).astype(BF16)
+        b_s[i] = exact(offsets[:, i * C : (i + 1) * C], e_s[...].astype(F32))
+    pw_s[...] = mul(e_s[...], projw[...], TN).astype(BF16)
 
     for copy in labels:
         copy.wait()
@@ -172,16 +197,26 @@
     )
     pick = ((iota((tile_cols, wins), 0) >> 3) == iota((tile_cols, wins), 1)).astype(F32)
     columns = exact(spread, pick)
-    tiled = (iota((SPAN, LANES), 0) == (iota((SPAN, LANES), 1) & (SPAN - 1))).astype(F32)
+    tiled = (iota((SPAN, LANE), 0) == (iota((SPAN, LANE), 1) & (SPAN - 1))).astype(F32)
     lab_row[...] = exact(columns, tiled, TN)
     for w in range(wins):
         lab_col[w] = jnp.broadcast_to(columns[:, w : w + 1], (SPAN, 128))
 
+    lane = iota((SPAN, LANE), 1)
+
     def gather_heads(stacked):
-        kept = stacked * hmask[...].astype(F32)
-        return jnp.sum(kept.reshape(HEADS, SPAN, C), 0)
-
-    small = 4 * BLOCK
+        out = stacked[-SPAN:]
+        for h in range(stacked.shape[0] // SPAN - 2, -1, -1):
+            out = jnp.where(lane < (h + 1) * HEADW, stacked[h * SPAN : (h + 1) * SPAN], out)
+        return out
+
+    def diagonal(x, heads):
+        tiles = x.reshape(SPAN // 16, 16, LANE)
+        parts = [
+            (tiles * hmask[h * 16 : (h + 1) * 16, :][None]).reshape(SPAN, LANE) for h in range(heads)
+        ]
+        return jnp.concatenate(parts, 0)
+
     edge = tile_cols - EDGE
     backs = []
 
@@ -227,40 +262,50 @@
         v_s[at] = (mul(n, w_s[2]) + b_s[2]).astype(BF16)
         g = gradf[win_at].reshape(step, C).astype(BF16)
         gb_s[at] = g
-        da_s[at] = mul(g, projw[...], NT).astype(BF16)
+        da_s[at] = mul(g, pw_s[...], NT).astype(BF16)
 
         @pl.loop(0, step_wins // 2)
         def _(pair_at):
-            loaded = []
             for i in range(2):
                 w = b * step_wins + pair_at * 2 + i
                 at = pl.ds(pl.multiple_of(w * SPAN, SPAN), SPAN)
-                same = lab_col[w][:, 0:1] == lab_row[pl.ds(w, 1), :]
-                loaded.append((at, q_s[at], k_s[at], v_s[at], da_s[at], same))
-            heads = hmask[...]
-            bias = bias_t[...]
-            total = score_acc[...]
-            for at, q, k, v, da, same in loaded:
-                qm = jnp.concatenate([q] * HEADS, 0) * heads
-                dam = jnp.concatenate([da] * HEADS, 0) * heads
-                scores = jnp.where(same, mul(k, qm, NT) + bias, MASKED)
-                e = jnp.exp(scores - jnp.max(scores, 0, keepdims=True))
-                p = e * (1.0 / jnp.sum(e, 0, keepdims=True))
-                p_low = p.astype(BF16)
-                att[at] = gather_heads(mul(p_low, v, TN)).astype(BF16)
-                dp = mul(v, dam, NT)
-                ds = p * (dp - jnp.sum(p * dp, 0, keepdims=True))
-                total += ds
-                ds_low = ds.astype(BF16)
-                dq_s[at] = (gather_heads(mul(ds_low, k, TN)) * HEAD ** (-0.5)).astype(BF16)
-                dk_s[at] = mul(ds_low, qm).astype(BF16)
-                dv_s[at] = mul(p_low, dam).astype(BF16)
-            score_acc[...] = total
+                same = lab_col[w] == lab_row[pl.ds(w, 1), :]
+                q, k, v, da = q_s[at], k_s[at], v_s[at], da_s[at]
+                att_w, dq_w, dk_w, dv_w = [], [], [], []
+                for lanes, heads in ((slice(0, LANE), 4), (slice(LANE, WIDE), 2)):
+                    kg, vg = k[:, lanes], v[:, lanes]
+                    qm, dam = diagonal(q[:, lanes], heads), diagonal(da[:, lanes], heads)
+                    scores = mul(kg, qm, NT)
+                    dp = mul(vg, dam, NT)
+                    lows, ds_lows = [], []
+                    for t in range(heads // 2):
+                        cut = slice(t * LANE, (t + 1) * LANE)
+                        out_at = slice(lanes.start + t * LANE, lanes.start + (t + 1) * LANE)
+                        if lanes.start:
+                            out_at = slice(WIDE, WIDE + LANE)
+                        biased = jnp.where(same, scores[:, cut] + bias_t[:, out_at], MASKED)
+                        e = jnp.exp(biased - jnp.max(biased, 0, keepdims=True))
+                        p = e * (1.0 / jnp.sum(e, 0, keepdims=True))
+                        lows.append(p.astype(BF16))
+                        grad = dp[:, cut]
+                        ds = p * (grad - jnp.sum(p * grad, 0, keepdims=True))
+                        score_acc[:, out_at] += ds
+                        ds_lows.append(ds.astype(BF16))
+                    p_low = jnp.concatenate(lows, 1)
+                    ds_low = jnp.concatenate(ds_lows, 1)
+                    att_w.append(gather_heads(mul(p_low, vg, TN)).astype(BF16))
+                    dq_w.append((gather_heads(mul(ds_low, kg, TN)) * HEAD ** (-0.5)).astype(BF16))
+                    dk_w.append(mul(ds_low, qm).astype(BF16))
+                    dv_w.append(mul(p_low, dam).astype(BF16))
+                att[at] = jnp.concatenate(att_w, 1)
+                dq_s[at] = jnp.concatenate(dq_w, 1)
+                dk_s[at] = jnp.concatenate(dk_w, 1)
+                dv_s[at] = jnp.concatenate(dv_w, 1)
 
         x = unit[win_at].reshape(step, C)
         dn = mul(dq_s[at], w_s[0], NT) + mul(dk_s[at], w_s[1], NT) + mul(dv_s[at], w_s[2], NT)
-        pack[small + 3 : small + 4, 0:C] += jnp.sum(dn * x, 0, keepdims=True)
-        pack[small + 4 : small + 5, 0:C] += jnp.sum(dn, 0, keepdims=True)
+        sums[0:1, 0:C] += jnp.sum(dn * x, 0, keepdims=True)
+        sums[1:2, 0:C] += jnp.sum(dn, 0, keepdims=True)
         g = dn * gain_ref[...]
         dx = inv_std[at] * (
             g - jnp.mean(g, -1, keepdims=True) - x * jnp.mean(g * x, -1, keepdims=True)
@@ -276,9 +321,17 @@
             back(frame_low.at[0:SHIFT, edge:tile_cols], back_l, row, other)
             back(frame_two.at[0:2, edge:tile_cols], back_ul, down, other)
 
+    lows = []
     for i, part in enumerate((dq_s, dk_s, dv_s)):
-        pack[i * BLOCK : (i + 1) * BLOCK, 0:C] = mul(nt_s[...], part[...])[0:BLOCK]
-    pack[3 * BLOCK : 3 * BLOCK + C, 0:C] = mul(att[...], gb_s[...], TN)
+        product = mul(nt_s[...], part[...])
+        pack[i * BLOCK : (i + 1) * BLOCK, :] = product[:, 0:LANE]
+        lows.append(product[:, LANE:WIDE])
+    product = mul(gb_s[...], att[...], TN)
+    pack[3 * BLOCK : 3 * BLOCK + C, :] = product[:, 0:LANE]
+    pack[3 * BLOCK + C : 4 * BLOCK, :] = jnp.zeros((BLOCK - C, LANE), F32)
+    pack[4 * BLOCK : 5 * BLOCK, :] = lows[0] + pltpu.roll(lows[1], 64, 1)
+    pack[5 * BLOCK : 6 * BLOCK, :] = lows[2]
+    pack[5 * BLOCK : 5 * BLOCK + C, :] += pltpu.roll(product[:, LANE:WIDE], 64, 1)
     for h in range(HEADS):
         span_a[h * SPAN : (h + 1) * SPAN, :] = score_acc[:, h * SPAN : (h + 1) * SPAN]
     wide = jnp.concatenate(
@@ -289,7 +342,9 @@
         [span_b[pl.ds(rj, HEADS, stride=WIN), :] for rj in range(WIN)], 1
     )
     flat_sum = split_mul(wide, fold_b[...])
-    pack[small + 8 : small + 8 + HEADS, :] = flat_sum
+    sums[8 : 8 + HEADS, :] = flat_sum
+    pack[small : small + 16, :] = sums[:, 0:LANE]
+    pack[small + 16 : small + 32, :] = sums[:, LANE:WIDE]
     pack_low[...] = pack[...].astype(BF16)
 
     pair = remote(
@@ -359,19 +414,22 @@
     def _(k):
         forward(k).wait()
 
-    pack[0:half] = result[0].astype(F32) * out_scale
-    pack[half : 2 * half] = result[1].astype(F32) * out_scale
-    d_qkvw[...] = jnp.concatenate(
-        [pack[i * BLOCK : i * BLOCK + C, 0:C] for i in range(3)], 1
-    )
-    d_qkvb[...] = jnp.concatenate(
-        [pack[i * BLOCK + C : i * BLOCK + C + 1, 0:C] for i in range(3)], 1
-    )
-    d_projw[...] = pack[3 * BLOCK : 3 * BLOCK + C, 0:C]
-    d_gain[...] = pack[small + 3 : small + 4, 0:C]
-    d_offset[...] = pack[small + 4 : small + 5, 0:C]
+    done = jnp.concatenate([result[0], result[1]], 0)
+    blocks = [done[i * BLOCK : (i + 1) * BLOCK] for i in range(6)]
+    joined = jnp.concatenate([blocks[i] for i in (0, 1, 2, 4, 5)], 1)
+    product = mul(joined, pick_s[...]) * out_scale
+    d_qkvw[...] = product[0:C]
+    d_qkvb[...] = product[C : C + 1]
+    spread = e_s[...]
+    far = pltpu.roll(spread[:, LANE:WIDE].astype(F32), 64, 1).astype(BF16)
+    product = mul(spread[:, 0:LANE], blocks[3], NT) + mul(far, blocks[5], NT)
+    d_projw[...] = product[:, 0:C] * out_scale
+    tail = done[small : small + 32].astype(F32) * out_scale
+    tail = jnp.concatenate([tail[0:16], tail[16:32]], 1)
+    d_gain[...] = tail[0:1, 0:C]
+    d_offset[...] = tail[1:2, 0:C]
     entries = table_spread(d_table.shape[1])
-    d_table[...] = exact(pack[small + 8 : small + 8 + HEADS, :], entries, NT)
+    d_table[...] = exact(tail[8 : 8 + HEADS, :], entries, NT)
 
 
 def on_device(
@@ -383,7 +441,7 @@
     count = wins * SPAN
     steps = wins // 4
     unit_rows = 2 * 16 * rows_n
-    needed = 4 * BLOCK + 16
+    needed = 6 * BLOCK + 32
     rows_total = -(-needed // unit_rows) * unit_rows
     half = rows_total // 2
     chunk = half // rows_n
@@ -401,7 +459,7 @@
         vmem((SHIFT, EDGE, C), BF16),
         vmem((2, EDGE, 2 * C), BF16),
     ]
-    flat_low = vmem((count, C), BF16)
+    flat_low = vmem((count, WIDE), BF16)
     whole = pl.BlockSpec(memory_space=pltpu.VMEM)
     dma = pltpu.SemaphoreType.DMA
     outs = pl.pallas_call(
@@ -424,25 +482,29 @@
             vmem((count, 1), F32),
             vmem((wins, WIN, WIN, C), F32),
             vmem((192, count), BF16),
-        ] + [flat_low] * 9 + [
-            vmem((3, C, C), BF16),
-            vmem((3, 1, C), F32),
+        ] + [flat_low] * 4 + [vmem((count, C), BF16)] + [flat_low] * 4 + [
+            vmem((3, C, WIDE), BF16),
+            vmem((3, 1, WIDE), F32),
+            vmem((WIDE, C), BF16),
+            vmem((C, WIDE), BF16),
+            vmem((5 * LANE, 3 * C), BF16),
             vmem((SPAN, LANES), F32),
             vmem((HEADS * SPAN, SPAN), F32),
             vmem((HEADS * WIN, 128), F32),
-            vmem((LANES, C), BF16),
+            vmem((4 * 16, LANE), BF16),
             vmem((wins, SPAN, 128), F32),
-            vmem((wins, LANES), F32),
+            vmem((wins, LANE), F32),
             vmem((SPAN, LANES), F32),
+            vmem((16, WIDE), F32),
             vmem((WIN * SPAN, 128), BF16),
             vmem((WIN * 128, 256), BF16),
         ] + home + [
-            vmem((rows_total, 256), F32),
-            vmem((rows_total, 256), BF16),
-            vmem((half, 256), BF16),
-            vmem((half, 256), BF16),
-            vmem((rows_n, chunk, 256), BF16),
-            vmem((2, half, 256), BF16),
+            vmem((rows_total, LANE), F32),
+            vmem((rows_total, LANE), BF16),
+            vmem((half, LANE), BF16),
+            vmem((half, LANE), BF16),
+            vmem((rows_n, chunk, LANE), BF16),
+            vmem((2, half, LANE), BF16),
             dma((4 + steps,)), dma((4 + steps,)),
             dma((steps + 2,)), dma((steps + 2,)), dma((2,)),
             dma((rows_n,)), dma((rows_n,)), dma((rows_n,)), dma((rows_n,)),

time: 52.4 us -> 51.4 us (0.981)
  Pallas kernels: 43.5 us -> 42.5 us
    pallas_call x1, Pallas kernels: 43.5 us -> 42.5 us  [on_device(): pl.pallas_call(functools.partial(body, rows_n, cols_n, rows_total, total_...]
where the time goes in v1:
time: 51.4 us; the launch traced here: 51.3 us
  Pallas kernels  42.5 us (83%)
  local copies, waits for them, and re-layouts  7.11 us (14%)
  other arithmetic  0.91 us (2%)
  between operations  0.73 us (1%)
    pallas_call x1, Pallas kernels, on_device(): pl.pallas_call(functools.partial(body, rows_n, cols_n, rows_total, total_...  42.5 us
    unnamed x22, local copies, waits for them, and re-layouts  6.38 us

profile of v1, /device:TPU:0, one launch (start us, length us, event | category | flops | bytes accessed | tf_op | source)
XLA Modules:
  0.0 51.3 jit_solution(10064858727906088294)
XLA Ops:
  0.6 0.0 copy-start.6
  0.6 0.7 %reshape.34.qkvb = f32[1,540]{1,0:T(1,128)S(1)} reshape(f32[540]{0:T(1024)} %param.15) | data formatting | bytes 4320 | tf_op jit(solution)/shard_map/reshape | solution.py:518
  1.4 1.2 %copy.16 = bf16[8,128,180]{2,1,0:T(8,128)(2,1)S(1)} copy(bf16[8,128,180]{1,0,2:T(8,128)(2,1)} %param.9) | data formatting | bytes 737280 | tf_op args[0]
  2.6 0.0 copy-done.6
  2.6 0.3 copy.17
  2.9 0.0 copy-start
  3.0 0.0 copy-start.1
  3.0 0.0 copy-start.2
  3.0 0.0 copy-start.3
  3.0 0.0 copy-start.4
  3.0 0.0 copy-start.5
  3.0 0.3 pad_maximum_fusion.both
  3.3 0.6 %copy-done = bf16[180,540]{1,0:T(8,128)(2,1)S(1)} copy-done((bf16[180,540]{1,0:T(8,128)(2,1)S(1)}, bf16[180,540]{1,0:T(8,128)(2,1)}, u32[]{:S(2)}) %copy-start) | copy-done | bytes 194424
  3.9 0.1 copy-done.1
  4.0 0.0 copy-done.2
  4.0 0.0 copy-done.3
  4.0 0.0 copy-done.4
  4.0 0.0 copy-done.5
  4.0 42.5 %shard_map.144 = (bf16[8,128,180]{2,1,0:T(8,128)(2,1)S(1)}, f32[180,540]{1,0:T(8,128)S(1)}, f32[1,540]{1,0:T(1,128)S(1)}, f32[180,180]{1,0:T(8,128)S(1)}, f32[6,...) custom-call(bf16[8,128,360]{2,1,0:T(8,128)(2,1)S(1)} %pad_maximum_fusion.both, s32[8,128]{1,0:T(8,128)S(1)} %copy-done.3, ...), custom_call_target="tpu_custom_call" | custom-call | tf_op jit(solution)/shard_map/pallas_call | solution.py:465
  46.5 1.0 %copy.18 = bf16[8,128,180]{1,0,2:T(8,128)(2,1)} copy(bf16[8,128,180]{2,1,0:T(8,128)(2,1)S(1)} %get-tuple-element.21) | data formatting | bytes 737280
  47.5 0.6 %reduce = f32[540]{0:T(1024)} reduce(f32[1,540]{1,0:T(1,128)S(1)} %get-tuple-element.16, f32[]{:T(128)} %constant.3), dimensions={0}, to_apply=%get-tuple-element.16.reduce_sub_computation | reduce | bytes 4324 | tf_op jit(solution)/shard_map/pallas_call | solution.py:465
  48.1 0.8 %copy.24 = f32[180,540]{1,0:T(8,128)} copy(f32[180,540]{1,0:T(8,128)S(1)} %get-tuple-element.36) | data formatting | bytes 777600
  48.9 0.7 %copy.25 = f32[180,180]{1,0:T(8,128)} copy(f32[180,180]{1,0:T(8,128)S(1)} %get-tuple-element.38) | data formatting | bytes 259200
  49.5 0.6 %copy.26 = f32[225,6]{0,1:T(8,128)} copy(f32[225,6]{0,1:T(8,128)S(1)} %bitcast.7) | data formatting | bytes 10800
  50.1 0.6 %copy.27 = f32[180]{0:T(256)} copy(f32[180]{0:T(256)S(1)} %bitcast.9) | data formatting | bytes 1440
  50.7 0.6 %copy.28 = f32[180]{0:T(256)} copy(f32[180]{0:T(256)S(1)} %bitcast.8) | data formatting | bytes 1440
Async XLA Ops:
  0.6 2.0 %copy-start.6 = (bf16[8,128,180]{1,0,2:T(8,128)(2,1)S(1)}, bf16[8,128,180]{1,0,2:T(8,128)(2,1)}, u32[]{:S(2)}) copy-start(bf16[8,128,180]{1,0,2:T(8,128)(2,1)} %param.10) | copy-start | bytes 1105924
  2.9 0.9 %copy-start = (bf16[180,540]{1,0:T(8,128)(2,1)S(1)}, bf16[180,540]{1,0:T(8,128)(2,1)}, u32[]{:S(2)}) copy-start(bf16[180,540]{1,0:T(8,128)(2,1)} %qkvw.1) | copy-start | bytes 583204
  3.0 1.0 %copy-start.1 = (bf16[180,180]{1,0:T(8,128)(2,1)S(1)}, bf16[180,180]{1,0:T(8,128)(2,1)}, u32[]{:S(2)}) copy-start(bf16[180,180]{1,0:T(8,128)(2,1)} %projw.1) | copy-start | bytes 194404
  3.0 1.0 %copy-start.2 = (f32[225,6]{0,1:T(8,128)S(1)}, f32[225,6]{0,1:T(8,128)}, u32[]{:S(2)}) copy-start(f32[225,6]{0,1:T(8,128)} %param.17) | copy-start | bytes 16204
  3.0 1.0 %copy-start.3 = (s32[8,128]{1,0:T(8,128)S(1)}, s32[8,128]{1,0:T(8,128)}, u32[]{:S(2)}) copy-start(s32[8,128]{1,0:T(8,128)} %reg.1) | copy-start | bytes 12292
  3.0 1.0 %copy-start.4 = (f32[180]{0:T(256)S(1)}, f32[180]{0:T(256)}, u32[]{:S(2)}) copy-start(f32[180]{0:T(256)} %param.12) | copy-start | bytes 2164
  3.0 1.0 %copy-start.5 = (f32[180]{0:T(256)S(1)}, f32[180]{0:T(256)}, u32[]{:S(2)}) copy-start(f32[180]{0:T(256)} %param.13) | copy-start | bytes 2164

commit v2 on v1

--- a/solution.py
+++ b/solution.py
@@ -95,6 +95,7 @@
     both_b, both_r, both_d, reg_b, reg_r,
     unit, inv_std, gradf, nt_s, q_s, k_s, v_s, da_s, gb_s, att, dq_s, dk_s, dv_s,
     w_s, b_s, pw_s, e_s, pick_s, bias_t, span_a, span_b, hmask, lab_col, lab_row, score_acc, sums,
+    scores_s, dp_s, p_s, ds_s,
     fold_a, fold_b, frame_low, frame_two, back_u, back_l, back_ul,
     pack, pack_low, pair_in, half_low, part_in, result,
     halo_send, halo_recv, back_send, back_recv, pair_sem,
@@ -217,6 +218,40 @@
         ]
         return jnp.concatenate(parts, 0)
 
+    groups = ((slice(0, LANE), slice(0, 4 * SPAN), 4), (slice(LANE, WIDE), slice(4 * SPAN, LANES), 2))
+
+    def score_step(w0, n):
+        for w in range(w0, w0 + n):
+            at = slice(w * SPAN, (w + 1) * SPAN)
+            for lanes, cut, heads in groups:
+                scores_s[w, :, cut] = mul(k_s[at, lanes], diagonal(q_s[at, lanes], heads), NT)
+                dp_s[w, :, cut] = mul(v_s[at, lanes], diagonal(da_s[at, lanes], heads), NT)
+
+    def softmax_step(w0, n):
+        for w in range(w0, w0 + n):
+            same = lab_col[w] == lab_row[w : w + 1, :]
+            for t in range(HEADS // 2):
+                cut = slice(t * LANE, (t + 1) * LANE)
+                scores = jnp.where(same, scores_s[w, :, cut] + bias_t[:, cut], MASKED)
+                e = jnp.exp(scores - jnp.max(scores, 0, keepdims=True))
+                p = e * (1.0 / jnp.sum(e, 0, keepdims=True))
+                p_s[w, :, cut] = p.astype(BF16)
+                dp = dp_s[w, :, cut]
+                ds = p * (dp - jnp.sum(p * dp, 0, keepdims=True))
+                score_acc[:, cut] += ds
+                ds_s[w, :, cut] = ds.astype(BF16)
+
+    def spread_step(w0, n):
+        for w in range(w0, w0 + n):
+            at = slice(w * SPAN, (w + 1) * SPAN)
+            for lanes, cut, heads in groups:
+                p, ds = p_s[w, :, cut], ds_s[w, :, cut]
+                att[at, lanes] = gather_heads(mul(p, v_s[at, lanes], TN)).astype(BF16)
+                dq = gather_heads(mul(ds, k_s[at, lanes], TN))
+                dq_s[at, lanes] = (dq * HEAD ** (-0.5)).astype(BF16)
+                dk_s[at, lanes] = mul(ds, diagonal(q_s[at, lanes], heads)).astype(BF16)
+                dv_s[at, lanes] = mul(p, diagonal(da_s[at, lanes], heads)).astype(BF16)
+
     edge = tile_cols - EDGE
     backs = []
 
@@ -264,43 +299,13 @@
         gb_s[at] = g
         da_s[at] = mul(g, pw_s[...], NT).astype(BF16)
 
-        @pl.loop(0, step_wins // 2)
-        def _(pair_at):
-            for i in range(2):
-                w = b * step_wins + pair_at * 2 + i
-                at = pl.ds(pl.multiple_of(w * SPAN, SPAN), SPAN)
-                same = lab_col[w] == lab_row[pl.ds(w, 1), :]
-                q, k, v, da = q_s[at], k_s[at], v_s[at], da_s[at]
-                att_w, dq_w, dk_w, dv_w = [], [], [], []
-                for lanes, heads in ((slice(0, LANE), 4), (slice(LANE, WIDE), 2)):
-                    kg, vg = k[:, lanes], v[:, lanes]
-                    qm, dam = diagonal(q[:, lanes], heads), diagonal(da[:, lanes], heads)
-                    scores = mul(kg, qm, NT)
-                    dp = mul(vg, dam, NT)
-                    lows, ds_lows = [], []
-                    for t in range(heads // 2):
-                        cut = slice(t * LANE, (t + 1) * LANE)
-                        out_at = slice(lanes.start + t * LANE, lanes.start + (t + 1) * LANE)
-                        if lanes.start:
-                            out_at = slice(WIDE, WIDE + LANE)
-                        biased = jnp.where(same, scores[:, cut] + bias_t[:, out_at], MASKED)
-                        e = jnp.exp(biased - jnp.max(biased, 0, keepdims=True))
-                        p = e * (1.0 / jnp.sum(e, 0, keepdims=True))
-                        lows.append(p.astype(BF16))
-                        grad = dp[:, cut]
-                        ds = p * (grad - jnp.sum(p * grad, 0, keepdims=True))
-                        score_acc[:, out_at] += ds
-                        ds_lows.append(ds.astype(BF16))
-                    p_low = jnp.concatenate(lows, 1)
-                    ds_low = jnp.concatenate(ds_lows, 1)
-                    att_w.append(gather_heads(mul(p_low, vg, TN)).astype(BF16))
-                    dq_w.append((gather_heads(mul(ds_low, kg, TN)) * HEAD ** (-0.5)).astype(BF16))
-                    dk_w.append(mul(ds_low, qm).astype(BF16))
-                    dv_w.append(mul(p_low, dam).astype(BF16))
-                att[at] = jnp.concatenate(att_w, 1)
-                dq_s[at] = jnp.concatenate(dq_w, 1)
-                dk_s[at] = jnp.concatenate(dk_w, 1)
-                dv_s[at] = jnp.concatenate(dv_w, 1)
+        first = b * step_wins
+        score_step(first, 2)
+        for w in range(first, first + step_wins, 2):
+            softmax_step(w, 2)
+            if w + 2 < first + step_wins:
+                score_step(w + 2, 2)
+            spread_step(w, 2)
 
         x = unit[win_at].reshape(step, C)
         dn = mul(dq_s[at], w_s[0], NT) + mul(dk_s[at], w_s[1], NT) + mul(dv_s[at], w_s[2], NT)
@@ -496,6 +501,10 @@
             vmem((wins, LANE), F32),
             vmem((SPAN, LANES), F32),
             vmem((16, WIDE), F32),
+            vmem((wins, SPAN, LANES), F32),
+            vmem((wins, SPAN, LANES), F32),
+            vmem((wins, SPAN, LANES), BF16),
+            vmem((wins, SPAN, LANES), BF16),
             vmem((WIN * SPAN, 128), BF16),
             vmem((WIN * 128, 256), BF16),
         ] + home + [

time: 51.4 us -> 45.3 us (0.88)
  Pallas kernels: 42.5 us -> 36.3 us
    pallas_call x1, Pallas kernels: 42.5 us -> 36.3 us  [on_device(): pl.pallas_call(functools.partial(body, rows_n, cols_n, rows_total, total_...]
where the time goes in v2:
time: 45.3 us; the launch traced here: 45.1 us
  Pallas kernels  36.3 us (80%)
  local copies, waits for them, and re-layouts  7.11 us (16%)
  other arithmetic  0.91 us (2%)
  between operations  0.73 us (2%)
    pallas_call x1, Pallas kernels, on_device(): pl.pallas_call(functools.partial(body, rows_n, cols_n, rows_total, total_...  36.3 us
    unnamed x22, local copies, waits for them, and re-layouts  6.38 us

profile of v2, /device:TPU:0, one launch (start us, length us, event | category | flops | bytes accessed | tf_op | source)
XLA Modules:
  0.0 45.1 jit_solution(16195886614871981545)
XLA Ops:
  0.6 0.0 copy-start.6
  0.6 0.7 %reshape.34.qkvb = f32[1,540]{1,0:T(1,128)S(1)} reshape(f32[540]{0:T(1024)} %param.15) | data formatting | bytes 4320 | tf_op jit(solution)/shard_map/reshape | solution.py:527
  1.4 1.2 %copy.16 = bf16[8,128,180]{2,1,0:T(8,128)(2,1)S(1)} copy(bf16[8,128,180]{1,0,2:T(8,128)(2,1)} %param.9) | data formatting | bytes 737280 | tf_op args[0]
  2.6 0.0 copy-done.6
  2.6 0.3 copy.17
  2.9 0.0 copy-start
  3.0 0.0 copy-start.1
  3.0 0.0 copy-start.2
  3.0 0.0 copy-start.3
  3.0 0.0 copy-start.4
  3.0 0.0 copy-start.5
  3.0 0.3 pad_maximum_fusion.both
  3.3 0.6 %copy-done = bf16[180,540]{1,0:T(8,128)(2,1)S(1)} copy-done((bf16[180,540]{1,0:T(8,128)(2,1)S(1)}, bf16[180,540]{1,0:T(8,128)(2,1)}, u32[]{:S(2)}) %copy-start) | copy-done | bytes 194424
  3.9 0.1 copy-done.1
  4.0 0.0 copy-done.2
  4.0 0.0 copy-done.3
  4.0 0.0 copy-done.4
  4.0 0.0 copy-done.5
  4.0 36.3 %shard_map.144 = (bf16[8,128,180]{2,1,0:T(8,128)(2,1)S(1)}, f32[180,540]{1,0:T(8,128)S(1)}, f32[1,540]{1,0:T(1,128)S(1)}, f32[180,180]{1,0:T(8,128)S(1)}, f32[6,...) custom-call(bf16[8,128,360]{2,1,0:T(8,128)(2,1)S(1)} %pad_maximum_fusion.both, s32[8,128]{1,0:T(8,128)S(1)} %copy-done.3, ...), custom_call_target="tpu_custom_call" | custom-call | tf_op jit(solution)/shard_map/pallas_call | solution.py:470
  40.3 1.0 %copy.18 = bf16[8,128,180]{1,0,2:T(8,128)(2,1)} copy(bf16[8,128,180]{2,1,0:T(8,128)(2,1)S(1)} %get-tuple-element.21) | data formatting | bytes 737280
  41.3 0.6 %reduce = f32[540]{0:T(1024)} reduce(f32[1,540]{1,0:T(1,128)S(1)} %get-tuple-element.16, f32[]{:T(128)} %constant.3), dimensions={0}, to_apply=%get-tuple-element.16.reduce_sub_computation | reduce | bytes 4324 | tf_op jit(solution)/shard_map/pallas_call | solution.py:470
  41.9 0.8 %copy.24 = f32[180,540]{1,0:T(8,128)} copy(f32[180,540]{1,0:T(8,128)S(1)} %get-tuple-element.36) | data formatting | bytes 777600
  42.7 0.7 %copy.25 = f32[180,180]{1,0:T(8,128)} copy(f32[180,180]{1,0:T(8,128)S(1)} %get-tuple-element.38) | data formatting | bytes 259200
  43.3 0.6 %copy.26 = f32[225,6]{0,1:T(8,128)} copy(f32[225,6]{0,1:T(8,128)S(1)} %bitcast.7) | data formatting | bytes 10800
  43.9 0.6 %copy.27 = f32[180]{0:T(256)} copy(f32[180]{0:T(256)S(1)} %bitcast.9) | data formatting | bytes 1440
  44.5 0.6 %copy.28 = f32[180]{0:T(256)} copy(f32[180]{0:T(256)S(1)} %bitcast.8) | data formatting | bytes 1440
Async XLA Ops:
  0.6 2.0 %copy-start.6 = (bf16[8,128,180]{1,0,2:T(8,128)(2,1)S(1)}, bf16[8,128,180]{1,0,2:T(8,128)(2,1)}, u32[]{:S(2)}) copy-start(bf16[8,128,180]{1,0,2:T(8,128)(2,1)} %param.10) | copy-start | bytes 1105924
  2.9 0.9 %copy-start = (bf16[180,540]{1,0:T(8,128)(2,1)S(1)}, bf16[180,540]{1,0:T(8,128)(2,1)}, u32[]{:S(2)}) copy-start(bf16[180,540]{1,0:T(8,128)(2,1)} %qkvw.1) | copy-start | bytes 583204
  3.0 1.0 %copy-start.1 = (bf16[180,180]{1,0:T(8,128)(2,1)S(1)}, bf16[180,180]{1,0:T(8,128)(2,1)}, u32[]{:S(2)}) copy-start(bf16[180,180]{1,0:T(8,128)(2,1)} %projw.1) | copy-start | bytes 194404
  3.0 1.0 %copy-start.2 = (f32[225,6]{0,1:T(8,128)S(1)}, f32[225,6]{0,1:T(8,128)}, u32[]{:S(2)}) copy-start(f32[225,6]{0,1:T(8,128)} %param.17) | copy-start | bytes 16204
  3.0 1.0 %copy-start.3 = (s32[8,128]{1,0:T(8,128)S(1)}, s32[8,128]{1,0:T(8,128)}, u32[]{:S(2)}) copy-start(s32[8,128]{1,0:T(8,128)} %reg.1) | copy-start | bytes 12292
  3.0 1.0 %copy-start.4 = (f32[180]{0:T(256)S(1)}, f32[180]{0:T(256)}, u32[]{:S(2)}) copy-start(f32[180]{0:T(256)} %param.12) | copy-start | bytes 2164
  3.0 1.0 %copy-start.5 = (f32[180]{0:T(256)S(1)}, f32[180]{0:T(256)}, u32[]{:S(2)}) copy-start(f32[180]{0:T(256)} %param.13) | copy-start | bytes 2164

commit v3 on v2

--- a/solution.py
+++ b/solution.py
@@ -90,7 +90,7 @@
 
 def body(
     rows_n, cols_n, rows_total, out_scale,
-    both, reg, gain_ref, offset_ref, qkvw, qkvb, projw, table,
+    both, reg, gain_in, offset_in, qkvw_in, qkvb_in, projw_in, table_in,
     d_tok, d_qkvw, d_qkvb, d_projw, d_table, d_gain, d_offset,
     both_b, both_r, both_d, reg_b, reg_r,
     unit, inv_std, gradf, nt_s, q_s, k_s, v_s, da_s, gb_s, att, dq_s, dk_s, dv_s,
@@ -98,6 +98,7 @@
     scores_s, dp_s, p_s, ds_s,
     fold_a, fold_b, frame_low, frame_two, back_u, back_l, back_ul,
     pack, pack_low, pair_in, half_low, part_in, result,
+    gain_ref, offset_ref, qkvw, qkvb, projw, table, local_sem,
     halo_send, halo_recv, back_send, back_recv, pair_sem,
     part_send, part_recv, all_send, all_recv, fwd_send, fwd_recv,
 ):
@@ -118,6 +119,15 @@
             device_id={"row": to_row, "col": to_col}, device_id_type=MESH,
         )
 
+    locals_ = [
+        pltpu.make_async_copy(src, dst, local_sem.at[i])
+        for i, (src, dst) in enumerate((
+            (table_in, table), (gain_in, gain_ref), (offset_in, offset_ref),
+            (qkvw_in, qkvw), (qkvb_in, qkvb), (projw_in, projw),
+        ))
+    ]
+    for copy in locals_:
+        copy.start()
     barrier = pltpu.get_barrier_semaphore()
 
     @pl.loop(1, rows_n)
@@ -156,6 +166,8 @@
     for copy in labels + chunks[0] + sides + chunks[1]:
         copy.start()
 
+    for copy in locals_:
+        copy.wait()
     flat = exact(table[...], table_spread(table.shape[1]))
     for rj in range(WIN):
         span_b[pl.ds(rj, HEADS, stride=WIN), :] = exact(flat, row_spread(rj), NT)
@@ -177,7 +189,7 @@
     for rj in range(WIN):
         fold_b[rj * 128 : (rj + 1) * 128, :] = row_spread(rj).astype(BF16)
     weights = qkvw[...]
-    offsets = qkvb[...]
+    offsets = qkvb[...].reshape(1, 3 * C)
     for i in range(3):
         w_s[i] = mul(weights[:, i * C : (i + 1) * C], e_s[...]).astype(BF16)
         b_s[i] = exact(offsets[:, i * C : (i + 1) * C], e_s[...].astype(F32))
@@ -435,6 +447,19 @@
     d_offset[...] = tail[1:2, 0:C]
     entries = table_spread(d_table.shape[1])
     d_table[...] = exact(tail[8 : 8 + HEADS, :], entries, NT)
+
+
+def finish(qkvw, qkvb, projw, table, gain, offset, *rest):
+    outs, flat, sems = rest[0:6], rest[6], rest[7]
+    flat[...] = qkvb[...].reshape(qkvb.shape[1])
+    sources = (qkvw, flat, projw, table, gain, offset)
+    copies = [
+        pltpu.make_async_copy(src, dst, sems.at[i]) for i, (src, dst) in enumerate(zip(sources, outs))
+    ]
+    for copy in copies:
+        copy.start()
+    for copy in copies:
+        copy.wait()
 
 
 def on_device(
@@ -478,7 +503,7 @@
             jax.ShapeDtypeStruct((1, C), F32),
             jax.ShapeDtypeStruct((1, C), F32),
         ),
-        in_specs=[whole] * 8,
+        in_specs=[whole] * 2 + [pl.BlockSpec(memory_space=pl.ANY)] * 6,
         out_specs=(whole,) * 7,
         scratch_shapes=halo + [
             vmem(regions.shape, jnp.int32),
@@ -514,6 +539,8 @@
             vmem((half, LANE), BF16),
             vmem((rows_n, chunk, LANE), BF16),
             vmem((2, half, LANE), BF16),
+            vmem((1, C), F32), vmem((1, C), F32), vmem(qkv_weight.shape, BF16), vmem((3 * C,), F32),
+            vmem(proj_weight.shape, BF16), vmem(bias_table.shape[::-1], F32), dma((6,)),
             dma((4 + steps,)), dma((4 + steps,)),
             dma((steps + 2,)), dma((steps + 2,)), dma((2,)),
             dma((rows_n,)), dma((rows_n,)), dma((rows_n,)), dma((rows_n,)),
@@ -524,13 +551,24 @@
         ),
     )(
         jnp.concatenate([tokens, grad_out], -1), regions, ln_gain.reshape(1, C), ln_offset.reshape(1, C), qkv_weight,
-        qkv_bias.reshape(1, 3 * C), proj_weight, bias_table.T,
-    )
-    d_tokens, d_qkvw, d_qkvb, d_projw, d_table, d_gain, d_offset = outs
+        qkv_bias, proj_weight, bias_table.T,
+    )
+    d_tokens = outs[0]
+    shapes = [jax.ShapeDtypeStruct(x.shape, F32) for x in outs[1:]]
+    shapes[1] = jax.ShapeDtypeStruct((3 * C,), F32)
+    anywhere = pl.BlockSpec(memory_space=pl.ANY)
+    d_qkvw, d_qkvb, d_projw, d_table, d_gain, d_offset = pl.pallas_call(
+        finish,
+        out_shape=shapes,
+        in_specs=[whole] * 6,
+        out_specs=[anywhere] * 6,
+        scratch_shapes=[vmem((3 * C,), F32), dma((6,))],
+        compiler_params=pltpu.CompilerParams(vmem_limit_bytes=1024 * 1024),
+    )(*outs[1:])
     return (
         d_tokens,
         d_qkvw,
-        d_qkvb.reshape(3 * C),
+        d_qkvb,
         d_projw,
         d_table.T,
         d_gain.reshape(C),

time: 45.3 us -> 42.1 us (0.929)
  local copies, waits for them, and re-layouts: 7.11 us -> 3.25 us
  Pallas kernels: 36.3 us -> 37.7 us
  other arithmetic: 0.91 us -> 0.3 us
    unnamed x22 -> x19, local copies, waits for them, and re-layouts: 6.38 us -> 3.25 us
    pallas_call x0 -> x1, Pallas kernels: none -> 0.89 us  [on_device(): pl.pallas_call(finish, out_shape=shapes, in_specs=[whole] * 6, out_specs=...]
    reshape x1 -> x0, local copies, waits for them, and re-layouts: 0.74 us -> none  [on_device(): qkv_bias.reshape(1, 3 * C)]
    pallas_call x1 -> x0, other arithmetic: 0.6 us -> none  [on_device(): pl.pallas_call(functools.partial(body, rows_n, cols_n, rows_total, total_...]
    pallas_call x1, Pallas kernels: 36.3 us -> 36.8 us  [on_device(): pl.pallas_call(functools.partial(body, rows_n, cols_n, rows_total, total_...]
where the time goes in v3:
time: 42.1 us; the launch traced here: 42 us
  Pallas kernels  37.7 us (90%)
  local copies, waits for them, and re-layouts  3.25 us (8%)
  between operations  0.74 us (2%)
    pallas_call x1, Pallas kernels, on_device(): pl.pallas_call(functools.partial(body, rows_n, cols_n, rows_total, total_...  36.8 us
    unnamed x19, local copies, waits for them, and re-layouts  3.25 us
    pallas_call x1, Pallas kernels, on_device(): pl.pallas_call(finish, out_shape=shapes, in_specs=[whole] * 6, out_specs=...  0.89 us

profile of v3, /device:TPU:0, one launch (start us, length us, event | category | flops | bytes accessed | tf_op | source)
XLA Modules:
  0.0 42.0 jit_solution(13507981297603162769)
XLA Ops:
  0.6 0.0 copy-start.7
  0.6 1.3 %copy.16 = bf16[8,128,180]{2,1,0:T(8,128)(2,1)S(1)} copy(bf16[8,128,180]{1,0,2:T(8,128)(2,1)} %param.9) | data formatting | bytes 737280 | tf_op args[0]
  1.9 0.0 copy-done.7
  1.9 0.3 copy.17
  2.2 0.0 copy-start
  2.3 0.0 copy-start.1
  2.3 0.0 copy-start.2
  2.3 0.0 copy-start.3
  2.3 0.0 copy-start.4
  2.3 0.0 copy-start.5
  2.3 0.0 copy-start.6
  2.3 0.3 pad_maximum_fusion.both
  2.6 0.6 %copy-done = bf16[180,540]{1,0:T(8,128)(2,1)S(1)} copy-done((bf16[180,540]{1,0:T(8,128)(2,1)S(1)}, bf16[180,540]{1,0:T(8,128)(2,1)}, u32[]{:S(2)}) %copy-start) | copy-done | bytes 194424
  3.2 0.1 copy-done.1
  3.3 0.0 copy-done.2
  3.3 0.0 copy-done.3
  3.3 0.0 copy-done.4
  3.3 0.0 copy-done.5
  3.3 0.0 copy-done.6
  3.3 36.8 %shard_map.144 = (bf16[8,128,180]{2,1,0:T(8,128)(2,1)S(1)}, f32[180,540]{1,0:T(8,128)S(1)}, f32[1,540]{1,0:T(1,128)S(1)}, f32[180,180]{1,0:T(8,128)S(1)}, f32[6,...) custom-call(bf16[8,128,360]{2,1,0:T(8,128)(2,1)S(1)} %pad_maximum_fusion.both, s32[8,128]{1,0:T(8,128)S(1)} %copy-done.3, ...), custom_call_target="tpu_custom_call" | custom-call | tf_op jit(solution)/shard_map/pallas_call | solution.py:495
  40.1 1.0 %copy.18 = bf16[8,128,180]{1,0,2:T(8,128)(2,1)} copy(bf16[8,128,180]{2,1,0:T(8,128)(2,1)S(1)} %get-tuple-element.33) | data formatting | bytes 737280
  41.1 0.9 %shard_map.145 = (f32[180,540]{1,0:T(8,128)}, f32[540]{0:T(1024)}, f32[180,180]{1,0:T(8,128)}, f32[6,225]{1,0:T(8,128)}, f32[1,180]{1,0:T(1,128)}, /*index=5*/f32[1,180]{1,0:T(1,128)}) custom-call(f32[180,540]{1,0:T(8,128)S(1)} %get-tuple-element.21.qkvw, f32[1,540]{1,0:T(1,128)S(1)} %get-tuple-element.22.qkvb, f32[180,180]{1,0:T(8,128)S(1)} %get-tuple-element.23.projw, ...), custom_call_target="tpu_custom_call" | custom-call | tf_op jit(solution)/shard_map/pallas_call | solution.py:560
Async XLA Ops:
  0.6 1.3 %copy-start.7 = (bf16[8,128,180]{1,0,2:T(8,128)(2,1)S(1)}, bf16[8,128,180]{1,0,2:T(8,128)(2,1)}, u32[]{:S(2)}) copy-start(bf16[8,128,180]{1,0,2:T(8,128)(2,1)} %param.10) | copy-start | bytes 1105924
  2.2 0.9 %copy-start = (bf16[180,540]{1,0:T(8,128)(2,1)S(1)}, bf16[180,540]{1,0:T(8,128)(2,1)}, u32[]{:S(2)}) copy-start(bf16[180,540]{1,0:T(8,128)(2,1)} %qkvw_in.1) | copy-start | bytes 583204
  2.3 1.0 %copy-start.1 = (bf16[180,180]{1,0:T(8,128)(2,1)S(1)}, bf16[180,180]{1,0:T(8,128)(2,1)}, u32[]{:S(2)}) copy-start(bf16[180,180]{1,0:T(8,128)(2,1)} %projw_in.1) | copy-start | bytes 194404
  2.3 1.0 %copy-start.2 = (f32[225,6]{0,1:T(8,128)S(1)}, f32[225,6]{0,1:T(8,128)}, u32[]{:S(2)}) copy-start(f32[225,6]{0,1:T(8,128)} %param.17) | copy-start | bytes 16204
  2.3 1.0 %copy-start.3 = (s32[8,128]{1,0:T(8,128)S(1)}, s32[8,128]{1,0:T(8,128)}, u32[]{:S(2)}) copy-start(s32[8,128]{1,0:T(8,128)} %reg.1) | copy-start | bytes 12292
  2.3 1.0 %copy-start.4 = (f32[540]{0:T(1024)S(1)}, f32[540]{0:T(1024)}, u32[]{:S(2)}) copy-start(f32[540]{0:T(1024)} %qkvb_in.1) | copy-start | bytes 6484
  2.3 1.0 %copy-start.5 = (f32[180]{0:T(256)S(1)}, f32[180]{0:T(256)}, u32[]{:S(2)}) copy-start(f32[180]{0:T(256)} %param.12) | copy-start | bytes 2164
  2.3 1.0 %copy-start.6 = (f32[180]{0:T(256)S(1)}, f32[180]{0:T(256)}, u32[]{:S(2)}) copy-start(f32[180]{0:T(256)} %param.13) | copy-start | bytes 2164

commit v4 on v3

--- a/solution.py
+++ b/solution.py
@@ -88,6 +88,10 @@
     return (iota((5 * LANE, 3 * C), 0) == wanted).astype(F32).astype(BF16)
 
 
+def window_steps(wins):
+    return [(w, 4) for w in range(wins - 4, 0, -4)] + [(2, 2), (0, 2)]
+
+
 def body(
     rows_n, cols_n, rows_total, out_scale,
     both, reg, gain_in, offset_in, qkvw_in, qkvb_in, projw_in, table_in,
@@ -95,7 +99,7 @@
     both_b, both_r, both_d, reg_b, reg_r,
     unit, inv_std, gradf, nt_s, q_s, k_s, v_s, da_s, gb_s, att, dq_s, dk_s, dv_s,
     w_s, b_s, pw_s, e_s, pick_s, bias_t, span_a, span_b, hmask, lab_col, lab_row, score_acc, sums,
-    scores_s, dp_s, p_s, ds_s,
+    scores_s, dp_s, p_s, ds_s, grads, turned,
     fold_a, fold_b, frame_low, frame_two, back_u, back_l, back_ul,
     pack, pack_low, pair_in, half_low, part_in, result,
     gain_ref, offset_ref, qkvw, qkvb, projw, table, local_sem,
@@ -143,27 +147,25 @@
         )
     pl.semaphore_wait(barrier, rows_n + 2)
 
-    step_wins = 4
-    step = step_wins * SPAN
-    steps = wins // step_wins
-    span_cols = step_wins * WIN
+    plan = window_steps(wins)
+    steps = len(plan)
 
     def halo(i, src, dst, to_row, to_col):
         return remote(src, dst, halo_send.at[i], halo_recv.at[i], to_row, to_col)
 
-    labels = [halo(0, reg, reg_b, up, col), halo(1, reg, reg_r, row, other)]
+    labels = [halo(0, reg, reg_b, down, col), halo(1, reg, reg_r, row, other)]
     sides = [
-        halo(2, both.at[SHIFT:WIN, 0:EDGE], both_r, row, other),
-        halo(3, both.at[0:SHIFT, 0:EDGE], both_d, up, other),
+        halo(2, both.at[0:SHIFT, 0:EDGE], both_r, row, other),
     ]
+    corner = halo(3, both.at[SHIFT:WIN, 0:EDGE], both_b.at[0:SHIFT, 0:EDGE], down, col)
+    corner_on = halo(4, both_b.at[0:SHIFT, 0:EDGE], both_d, row, other)
     chunks = []
-    for b in range(steps):
-        first = b * span_cols + (EDGE if b else 0)
-        last = min((b + 1) * span_cols + EDGE, tile_cols)
-        src, dst = both.at[0:SHIFT, first:last], both_b.at[0:SHIFT, first:last]
-        chunks.append([halo(4 + b, src, dst, up, col)])
+    for b, (w0, n) in enumerate(plan):
+        cols = slice(w0 * WIN, (w0 + n) * WIN)
+        chunks.append([halo(5 + b, both.at[SHIFT:WIN, cols], both_b.at[0:SHIFT, cols], down, col)] if w0 else [])
+    ahead = 9
     small = 6 * BLOCK
-    for copy in labels + chunks[0] + sides + chunks[1]:
+    for copy in labels + [corner] + sides + sum(chunks[:ahead], []):
         copy.start()
 
     for copy in locals_:
@@ -199,7 +201,7 @@
         copy.wait()
 
     own = reg[...]
-    row_part = jnp.concatenate([own[SHIFT:], reg_b[0:SHIFT, :]], 0)[:, 0:1] >> 2
+    row_part = jnp.concatenate([reg_b[SHIFT:, :], own[0:SHIFT]], 0)[:, 0:1] >> 2
     col_own = pltpu.roll(own, tile_cols - SHIFT, 1)
     col_right = pltpu.roll(reg_r[...], tile_cols - SHIFT, 1)
     col_part = jnp.where(iota((WIN, tile_cols), 1) < tile_cols - SHIFT, col_own, col_right)[0:1] & 3
@@ -272,24 +274,32 @@
         backs.append(remote(src, dst, back_send.at[i], back_recv.at[i], to_row, to_col))
         backs[-1].start()
 
-    for b in range(steps):
-        for copy in chunks[b] + (sides if b == steps - 1 else []):
+    corner.wait()
+    corner_on.start()
+    waiting = []
+    for b, (w0, step_wins) in enumerate(plan):
+        for copy in chunks[b] + ([] if b else sides + [corner_on]):
             copy.wait()
-        if b + 2 < steps:
-            for copy in chunks[b + 2]:
+        if b + ahead < steps:
+            for copy in chunks[b + ahead]:
                 copy.start()
-        at = slice(b * step, (b + 1) * step)
-        win_at = slice(b * step_wins, (b + 1) * step_wins)
-        cols = slice(b * span_cols, (b + 1) * span_cols)
-        near = slice(b * span_cols, min((b + 1) * span_cols + EDGE, tile_cols))
+        if b >= 2:
+            for copy in waiting:
+                back(*copy)
+            waiting = []
+        step, span_cols, end = step_wins * SPAN, step_wins * WIN, w0 + step_wins
+        at = slice(w0 * SPAN, end * SPAN)
+        win_at = slice(w0, end)
+        cols = slice(w0 * WIN, end * WIN)
+        near = slice(w0 * WIN, min(end * WIN + EDGE, tile_cols))
 
         for r in range(WIN):
             if r < SHIFT:
-                part, beyond = both[r + SHIFT, near], both_r[r]
+                part, beyond = both_b[r, near], both_d[r]
             else:
-                part, beyond = both_b[r - SHIFT, near], both_d[r - SHIFT]
+                part, beyond = both[r - SHIFT, near], both_r[r - SHIFT]
             wide = part.astype(F32)
-            if b == steps - 1:
+            if end == wins:
                 wide = jnp.concatenate([wide, beyond.astype(F32)], 0)
             wide = wide[SHIFT : SHIFT + span_cols]
             unit[win_at, r] = wide[:, 0:C].reshape(step_wins, WIN, C)
@@ -311,11 +321,10 @@
         gb_s[at] = g
         da_s[at] = mul(g, pw_s[...], NT).astype(BF16)
 
-        first = b * step_wins
-        score_step(first, 2)
-        for w in range(first, first + step_wins, 2):
+        score_step(w0, 2)
+        for w in range(w0, end, 2):
             softmax_step(w, 2)
-            if w + 2 < first + step_wins:
+            if w + 2 < end:
                 score_step(w + 2, 2)
             spread_step(w, 2)
 
@@ -329,26 +338,31 @@
         )
         out = (gradf[win_at].reshape(step, C) + dx).reshape(step_wins, WIN, WIN, C)
         for r in range(SHIFT):
-            frame_low[r, cols] = out[:, r].reshape(span_cols, C).astype(BF16)
+            frame_low[r, cols] = out[:, SHIFT + r].reshape(span_cols, C).astype(BF16)
         for r in range(0, SHIFT, 2):
-            two = [out[:, SHIFT + r + i].reshape(span_cols, C) for i in range(2)]
+            two = [out[:, r + i].reshape(span_cols, C) for i in range(2)]
             frame_two[r // 2, cols] = jnp.concatenate(two, 1).astype(BF16)
-        back(frame_two.at[0:2, cols], back_u.at[0:2, cols], down, col)
-        if b == steps - 1:
-            back(frame_low.at[0:SHIFT, edge:tile_cols], back_l, row, other)
-            back(frame_two.at[0:2, edge:tile_cols], back_ul, down, other)
-
-    lows = []
-    for i, part in enumerate((dq_s, dk_s, dv_s)):
-        product = mul(nt_s[...], part[...])
-        pack[i * BLOCK : (i + 1) * BLOCK, :] = product[:, 0:LANE]
-        lows.append(product[:, LANE:WIDE])
-    product = mul(gb_s[...], att[...], TN)
-    pack[3 * BLOCK : 3 * BLOCK + C, :] = product[:, 0:LANE]
+        waiting.append((frame_two.at[0:2, cols], back_u.at[0:2, cols], up, col))
+        if b == 0:
+            waiting.append((frame_low.at[0:SHIFT, edge:tile_cols], back_l, row, other))
+            waiting.append((frame_two.at[0:2, edge:tile_cols], back_ul, up, other))
+        if w0 != 2:
+            over = slice(w0 * SPAN, w0 * SPAN + 4 * SPAN)
+            for i, part in enumerate((dq_s, dk_s, dv_s)):
+                product = mul(nt_s[:, over], part[over])
+                grads[i] = product if b == 0 else grads[i] + product
+            product = mul(gb_s[over], att[over], TN)
+            grads[3, 0:C] = product if b == 0 else grads[3, 0:C] + product
+    for copy in waiting:
+        back(*copy)
+
+    for i in range(3):
+        pack[i * BLOCK : (i + 1) * BLOCK, :] = grads[i, :, 0:LANE]
+    pack[3 * BLOCK : 3 * BLOCK + C, :] = grads[3, 0:C, 0:LANE]
     pack[3 * BLOCK + C : 4 * BLOCK, :] = jnp.zeros((BLOCK - C, LANE), F32)
-    pack[4 * BLOCK : 5 * BLOCK, :] = lows[0] + pltpu.roll(lows[1], 64, 1)
-    pack[5 * BLOCK : 6 * BLOCK, :] = lows[2]
-    pack[5 * BLOCK : 5 * BLOCK + C, :] += pltpu.roll(product[:, LANE:WIDE], 64, 1)
+    pack[4 * BLOCK : 5 * BLOCK, :] = grads[0, :, LANE:WIDE] + pltpu.roll(grads[1, :, LANE:WIDE], 64, 1)
+    pack[5 * BLOCK : 6 * BLOCK, :] = grads[2, :, LANE:WIDE]
+    pack[5 * BLOCK : 5 * BLOCK + C, :] += pltpu.roll(grads[3, 0:C, LANE:WIDE], 64, 1)
     for h in range(HEADS):
         span_a[h * SPAN : (h + 1) * SPAN, :] = score_acc[:, h * SPAN : (h + 1) * SPAN]
     wide = jnp.concatenate(
@@ -384,18 +398,6 @@
     def _(k):
         part_copy(k).start()
 
-    for copy in backs:
-        copy.wait()
-    for r in range(WIN):
-        if r < SHIFT:
-            lanes = slice((r % 2) * C, (r % 2 + 1) * C)
-            left_part = back_ul[r // 2].astype(F32)[:, lanes]
-            main_part = back_u[r // 2].astype(F32)[:, lanes]
-        else:
-            left_part, main_part = back_l[r - SHIFT], frame_low[r - SHIFT]
-        wide = jnp.concatenate([left_part.astype(F32), main_part.astype(F32)], 0)
-        d_tok[r] = wide[EDGE - SHIFT : EDGE - SHIFT + tile_cols].astype(BF16)
-
     def add_part(k, total):
         part_copy(k).wait()
         return total + part_in[k].astype(F32)
@@ -421,6 +423,20 @@
         all_copy(k).start()
 
     forward(0).start()
+
+    for copy in backs:
+        copy.wait()
+    for r in range(WIN):
+        if r < SHIFT:
+            left_part, main_part = back_l[r], frame_low[r]
+        else:
+            lanes = slice((r % 2) * C, (r % 2 + 1) * C)
+            left_part = back_ul[(r - SHIFT) // 2].astype(F32)[:, lanes]
+            main_part = back_u[(r - SHIFT) // 2].astype(F32)[:, lanes]
+        wide = jnp.concatenate([left_part.astype(F32), main_part.astype(F32)], 0)
+        turned[pl.ds(r, C, stride=WIN), :] = wide[EDGE - SHIFT : EDGE - SHIFT + tile_cols].T
+    d_tok[...] = turned[...].reshape(C, WIN, tile_cols).astype(BF16)
+
 
     @pl.loop(1, rows_n)
     def _(k):
@@ -449,10 +465,10 @@
     d_table[...] = exact(tail[8 : 8 + HEADS, :], entries, NT)
 
 
-def finish(qkvw, qkvb, projw, table, gain, offset, *rest):
-    outs, flat, sems = rest[0:6], rest[6], rest[7]
+def finish(tok, qkvw, qkvb, projw, table, gain, offset, *rest):
+    outs, flat, sems = rest[0:7], rest[7], rest[8]
     flat[...] = qkvb[...].reshape(qkvb.shape[1])
-    sources = (qkvw, flat, projw, table, gain, offset)
+    sources = (tok, qkvw, flat, projw, table, gain, offset)
     copies = [
         pltpu.make_async_copy(src, dst, sems.at[i]) for i, (src, dst) in enumerate(zip(sources, outs))
     ]
@@ -469,7 +485,7 @@
     tile_cols = tokens.shape[1]
     wins = tile_cols // WIN
     count = wins * SPAN
-    steps = wins // 4
+    steps = len(window_steps(wins))
     unit_rows = 2 * 16 * rows_n
     needed = 6 * BLOCK + 32
     rows_total = -(-needed // unit_rows) * unit_rows
@@ -495,7 +511,7 @@
     outs = pl.pallas_call(
         functools.partial(body, rows_n, cols_n, rows_total, total_tokens ** (-0.5)),
         out_shape=(
-            jax.ShapeDtypeStruct(tokens.shape, BF16),
+            jax.ShapeDtypeStruct((C,) + tokens.shape[:2], BF16),
             jax.ShapeDtypeStruct((C, 3 * C), F32),
             jax.ShapeDtypeStruct((1, 3 * C), F32),
             jax.ShapeDtypeStruct((C, C), F32),
@@ -530,6 +546,8 @@
             vmem((wins, SPAN, LANES), F32),
             vmem((wins, SPAN, LANES), BF16),
             vmem((wins, SPAN, LANES), BF16),
+            vmem((4, BLOCK, WIDE), F32),
+            vmem((C * WIN, tile_cols), F32),
             vmem((WIN * SPAN, 128), BF16),
             vmem((WIN * 128, 256), BF16),
         ] + home + [
@@ -541,7 +559,7 @@
             vmem((2, half, LANE), BF16),
             vmem((1, C), F32), vmem((1, C), F32), vmem(qkv_weight.shape, BF16), vmem((3 * C,), F32),
             vmem(proj_weight.shape, BF16), vmem(bias_table.shape[::-1], F32), dma((6,)),
-            dma((4 + steps,)), dma((4 + steps,)),
+            dma((5 + steps,)), dma((5 + steps,)),
             dma((steps + 2,)), dma((steps + 2,)), dma((2,)),
             dma((rows_n,)), dma((rows_n,)), dma((rows_n,)), dma((rows_n,)),
             dma((rows_n,)), dma((rows_n,)),
@@ -553,20 +571,19 @@
         jnp.concatenate([tokens, grad_out], -1), regions, ln_gain.reshape(1, C), ln_offset.reshape(1, C), qkv_weight,
         qkv_bias, proj_weight, bias_table.T,
     )
-    d_tokens = outs[0]
-    shapes = [jax.ShapeDtypeStruct(x.shape, F32) for x in outs[1:]]
-    shapes[1] = jax.ShapeDtypeStruct((3 * C,), F32)
+    shapes = [jax.ShapeDtypeStruct(x.shape, x.dtype) for x in outs]
+    shapes[2] = jax.ShapeDtypeStruct((3 * C,), F32)
     anywhere = pl.BlockSpec(memory_space=pl.ANY)
-    d_qkvw, d_qkvb, d_projw, d_table, d_gain, d_offset = pl.pallas_call(
+    d_tokens, d_qkvw, d_qkvb, d_projw, d_table, d_gain, d_offset = pl.pallas_call(
         finish,
         out_shape=shapes,
-        in_specs=[whole] * 6,
-        out_specs=[anywhere] * 6,
-        scratch_shapes=[vmem((3 * C,), F32), dma((6,))],
+        in_specs=[whole] * 7,
+        out_specs=[anywhere] * 7,
+        scratch_shapes=[vmem((3 * C,), F32), dma((7,))],
         compiler_params=pltpu.CompilerParams(vmem_limit_bytes=1024 * 1024),
-    )(*outs[1:])
+    )(*outs)
     return (
-        d_tokens,
+        jnp.transpose(d_tokens, (1, 2, 0)),
         d_qkvw,
         d_qkvb,
         d_projw,

time: 42.1 us -> 40.6 us (0.964)
  local copies, waits for them, and re-layouts: 3.25 us -> 2.25 us
  Pallas kernels: 37.7 us -> 37.2 us
    unnamed x19 -> x18, local copies, waits for them, and re-layouts: 3.25 us -> 2.25 us
    pallas_call x1, Pallas kernels: 36.8 us -> 36.1 us  [on_device(): pl.pallas_call(functools.partial(body, rows_n, cols_n, rows_total, total_...]
where the time goes in v4:
time: 40.6 us; the launch traced here: 40.5 us
  Pallas kernels  37.2 us (92%)
  local copies, waits for them, and re-layouts  2.25 us (6%)
  between operations  0.74 us (2%)
    pallas_call x1, Pallas kernels, on_device(): pl.pallas_call(functools.partial(body, rows_n, cols_n, rows_total, total_...  36.1 us
    unnamed x18, local copies, waits for them, and re-layouts  2.25 us
    pallas_call x1, Pallas kernels, on_device(): pl.pallas_call(finish, out_shape=shapes, in_specs=[whole] * 7, out_specs=...  1.03 us

profile of v4, /device:TPU:0, one launch (start us, length us, event | category | flops | bytes accessed | tf_op | source)
XLA Modules:
  0.0 40.5 jit_solution(6836269265118858195)
XLA Ops:
  0.6 0.0 copy-start.7
  0.6 1.3 %copy.16 = bf16[8,128,180]{2,1,0:T(8,128)(2,1)S(1)} copy(bf16[8,128,180]{1,0,2:T(8,128)(2,1)} %param.9) | data formatting | bytes 737280 | tf_op args[0]
  1.9 0.0 copy-done.7
  1.9 0.3 copy.17
  2.2 0.0 copy-start
  2.3 0.0 copy-start.1
  2.3 0.0 copy-start.2
  2.3 0.0 copy-start.3
  2.3 0.0 copy-start.4
  2.3 0.0 copy-start.5
  2.3 0.0 copy-start.6
  2.3 0.3 pad_maximum_fusion.both
  2.6 0.6 %copy-done = bf16[180,540]{1,0:T(8,128)(2,1)S(1)} copy-done((bf16[180,540]{1,0:T(8,128)(2,1)S(1)}, bf16[180,540]{1,0:T(8,128)(2,1)}, u32[]{:S(2)}) %copy-start) | copy-done | bytes 194424
  3.2 0.1 copy-done.1
  3.3 0.0 copy-done.2
  3.3 0.0 copy-done.3
  3.3 0.0 copy-done.4
  3.3 0.0 copy-done.5
  3.3 0.0 copy-done.6
  3.3 36.1 %shard_map.144 = (bf16[180,8,128]{2,1,0:T(8,128)(2,1)S(1)}, f32[180,540]{1,0:T(8,128)S(1)}, f32[1,540]{1,0:T(1,128)S(1)}, f32[180,180]{1,0:T(8,128)S(1)}, f32[6,...) custom-call(bf16[8,128,360]{2,1,0:T(8,128)(2,1)S(1)} %pad_maximum_fusion.both, s32[8,128]{1,0:T(8,128)S(1)} %copy-done.3, ...), custom_call_target="tpu_custom_call" | custom-call | tf_op jit(solution)/shard_map/pallas_call | solution.py:511
  39.4 1.0 %shard_map.145 = (bf16[180,8,128]{2,1,0:T(8,128)(2,1)}, f32[180,540]{1,0:T(8,128)}, f32[540]{0:T(1024)}, f32[180,180]{1,0:T(8,128)}, f32[6,225]{1,0:T(8,128)}, /*index=5*/f32[1,180]{1,0:T(1,128)}, f32[1,180]{1,0:T(1,128)}) custom-call(bf16[180,8,128]{2,1,0:T(8,128)(2,1)S(1)} %get-tuple-element.21.tok, f32[180,540]{1,0:T(8,128)S(1)} %get-tuple-element.22.qkvw, ...), custom_call_target="tpu_custom_call" | custom-call | tf_op jit(solution)/shard_map/pallas_call | solution.py:577
Async XLA Ops:
  0.6 1.3 %copy-start.7 = (bf16[8,128,180]{1,0,2:T(8,128)(2,1)S(1)}, bf16[8,128,180]{1,0,2:T(8,128)(2,1)}, u32[]{:S(2)}) copy-start(bf16[8,128,180]{1,0,2:T(8,128)(2,1)} %param.10) | copy-start | bytes 1105924
  2.2 0.9 %copy-start = (bf16[180,540]{1,0:T(8,128)(2,1)S(1)}, bf16[180,540]{1,0:T(8,128)(2,1)}, u32[]{:S(2)}) copy-start(bf16[180,540]{1,0:T(8,128)(2,1)} %qkvw_in.1) | copy-start | bytes 583204
  2.3 1.0 %copy-start.1 = (bf16[180,180]{1,0:T(8,128)(2,1)S(1)}, bf16[180,180]{1,0:T(8,128)(2,1)}, u32[]{:S(2)}) copy-start(bf16[180,180]{1,0:T(8,128)(2,1)} %projw_in.1) | copy-start | bytes 194404
  2.3 1.0 %copy-start.2 = (f32[225,6]{0,1:T(8,128)S(1)}, f32[225,6]{0,1:T(8,128)}, u32[]{:S(2)}) copy-start(f32[225,6]{0,1:T(8,128)} %param.17) | copy-start | bytes 16204
  2.3 1.0 %copy-start.3 = (s32[8,128]{1,0:T(8,128)S(1)}, s32[8,128]{1,0:T(8,128)}, u32[]{:S(2)}) copy-start(s32[8,128]{1,0:T(8,128)} %reg.1) | copy-start | bytes 12292
  2.3 1.0 %copy-start.4 = (f32[540]{0:T(1024)S(1)}, f32[540]{0:T(1024)}, u32[]{:S(2)}) copy-start(f32[540]{0:T(1024)} %qkvb_in.1) | copy-start | bytes 6484
  2.3 1.0 %copy-start.5 = (f32[180]{0:T(256)S(1)}, f32[180]{0:T(256)}, u32[]{:S(2)}) copy-start(f32[180]{0:T(256)} %param.12) | copy-start | bytes 2164
  2.3 1.0 %copy-start.6 = (f32[180]{0:T(256)S(1)}, f32[180]{0:T(256)}, u32[]{:S(2)}) copy-start(f32[180]{0:T(256)} %param.13) | copy-start | bytes 2164

commit v5 on v4

--- a/solution.py
+++ b/solution.py
@@ -94,15 +94,15 @@
 
 def body(
     rows_n, cols_n, rows_total, out_scale,
-    both, reg, gain_in, offset_in, qkvw_in, qkvb_in, projw_in, table_in,
+    tok_in, grad_in, reg_in, gain_in, offset_in, qkvw_in, qkvb_in, projw_in, table_in,
     d_tok, d_qkvw, d_qkvb, d_projw, d_table, d_gain, d_offset,
-    both_b, both_r, both_d, reg_b, reg_r,
+    both, spread_t, both_b, both_r, both_d, reg_b, reg_r,
     unit, inv_std, gradf, nt_s, q_s, k_s, v_s, da_s, gb_s, att, dq_s, dk_s, dv_s,
     w_s, b_s, pw_s, e_s, pick_s, bias_t, span_a, span_b, hmask, lab_col, lab_row, score_acc, sums,
     scores_s, dp_s, p_s, ds_s, grads, turned,
     fold_a, fold_b, frame_low, frame_two, back_u, back_l, back_ul,
     pack, pack_low, pair_in, half_low, part_in, result,
-    gain_ref, offset_ref, qkvw, qkvb, projw, table, local_sem,
+    tok_t, grad_t, reg, gain_ref, offset_ref, qkvw, qkvb, projw, table, local_sem,
     halo_send, halo_recv, back_send, back_recv, pair_sem,
     part_send, part_recv, all_send, all_recv, fwd_send, fwd_recv,
 ):
@@ -111,7 +111,7 @@
     up = lax.rem(row + rows_n - 1, rows_n)
     down = lax.rem(row + 1, rows_n)
     other = lax.rem(col + 1, cols_n)
-    tile_cols = both.shape[1]
+    tile_cols = tok_in.shape[2]
     wins = tile_cols // WIN
     count = wins * SPAN
     half = rows_total // 2
@@ -126,6 +126,7 @@
     locals_ = [
         pltpu.make_async_copy(src, dst, local_sem.at[i])
         for i, (src, dst) in enumerate((
+            (tok_in, tok_t), (grad_in, grad_t), (reg_in, reg),
             (table_in, table), (gain_in, gain_ref), (offset_in, offset_ref),
             (qkvw_in, qkvw), (qkvb_in, qkvb), (projw_in, projw),
         ))
@@ -145,6 +146,15 @@
         pl.semaphore_signal(
             barrier, inc=1, device_id={"row": to_row, "col": other}, device_id_type=MESH
         )
+    def turn(r):
+        both[r] = spread_t[pl.ds(r, 2 * C, stride=WIN), :].T.astype(BF16)
+
+    for copy in locals_[0:3]:
+        copy.wait()
+    spread_t[0 : C * WIN, :] = tok_t[...].astype(F32).reshape(C * WIN, tile_cols)
+    spread_t[C * WIN : 2 * C * WIN, :] = grad_t[...].astype(F32).reshape(C * WIN, tile_cols)
+    for r in range(SHIFT, WIN):
+        turn(r)
     pl.semaphore_wait(barrier, rows_n + 2)
 
     plan = window_steps(wins)
@@ -165,10 +175,14 @@
         chunks.append([halo(5 + b, both.at[SHIFT:WIN, cols], both_b.at[0:SHIFT, cols], down, col)] if w0 else [])
     ahead = 9
     small = 6 * BLOCK
-    for copy in labels + [corner] + sides + sum(chunks[:ahead], []):
+    for copy in labels + [corner] + sum(chunks[:ahead], []):
         copy.start()
-
-    for copy in locals_:
+    for r in range(SHIFT):
+        turn(r)
+    for copy in sides:
+        copy.start()
+
+    for copy in locals_[3:]:
         copy.wait()
     flat = exact(table[...], table_spread(table.shape[1]))
     for rj in range(WIN):
@@ -452,7 +466,7 @@
     joined = jnp.concatenate([blocks[i] for i in (0, 1, 2, 4, 5)], 1)
     product = mul(joined, pick_s[...]) * out_scale
     d_qkvw[...] = product[0:C]
-    d_qkvb[...] = product[C : C + 1]
+    d_qkvb[...] = product[C : C + 1].reshape(3 * C)
     spread = e_s[...]
     far = pltpu.roll(spread[:, LANE:WIDE].astype(F32), 64, 1).astype(BF16)
     product = mul(spread[:, 0:LANE], blocks[3], NT) + mul(far, blocks[5], NT)
@@ -465,16 +479,16 @@
     d_table[...] = exact(tail[8 : 8 + HEADS, :], entries, NT)
 
 
-def finish(tok, qkvw, qkvb, projw, table, gain, offset, *rest):
-    outs, flat, sems = rest[0:7], rest[7], rest[8]
-    flat[...] = qkvb[...].reshape(qkvb.shape[1])
-    sources = (tok, qkvw, flat, projw, table, gain, offset)
-    copies = [
-        pltpu.make_async_copy(src, dst, sems.at[i]) for i, (src, dst) in enumerate(zip(sources, outs))
-    ]
-    for copy in copies:
+def finish(*refs):
+    sources, outs, held, sems = refs[0:7], refs[7:14], refs[14:21], refs[21]
+    into = [pltpu.make_async_copy(sources[i], held[i], sems.at[0, i]) for i in range(7)]
+    away = [pltpu.make_async_copy(held[i], outs[i], sems.at[1, i]) for i in range(7)]
+    for copy in into:
         copy.start()
-    for copy in copies:
+    for first, second in zip(into, away):
+        first.wait()
+        second.start()
+    for copy in away:
         copy.wait()
 
 
@@ -513,15 +527,18 @@
         out_shape=(
             jax.ShapeDtypeStruct((C,) + tokens.shape[:2], BF16),
             jax.ShapeDtypeStruct((C, 3 * C), F32),
-            jax.ShapeDtypeStruct((1, 3 * C), F32),
+            jax.ShapeDtypeStruct((3 * C,), F32),
             jax.ShapeDtypeStruct((C, C), F32),
             jax.ShapeDtypeStruct((HEADS, bias_table.shape[0]), F32),
             jax.ShapeDtypeStruct((1, C), F32),
             jax.ShapeDtypeStruct((1, C), F32),
         ),
-        in_specs=[whole] * 2 + [pl.BlockSpec(memory_space=pl.ANY)] * 6,
+        in_specs=[pl.BlockSpec(memory_space=pl.ANY)] * 9,
         out_specs=(whole,) * 7,
-        scratch_shapes=halo + [
+        scratch_shapes=[
+            vmem((WIN, tile_cols, 2 * C), BF16),
+            vmem((2 * C * WIN, tile_cols), F32),
+        ] + halo + [
             vmem(regions.shape, jnp.int32),
             vmem(regions.shape, jnp.int32),
             vmem((wins, WIN, WIN, C), F32),
@@ -557,30 +574,30 @@
             vmem((half, LANE), BF16),
             vmem((rows_n, chunk, LANE), BF16),
             vmem((2, half, LANE), BF16),
+            vmem((C,) + tokens.shape[:2], BF16), vmem((C,) + tokens.shape[:2], BF16),
+            vmem(regions.shape, jnp.int32),
             vmem((1, C), F32), vmem((1, C), F32), vmem(qkv_weight.shape, BF16), vmem((3 * C,), F32),
-            vmem(proj_weight.shape, BF16), vmem(bias_table.shape[::-1], F32), dma((6,)),
+            vmem(proj_weight.shape, BF16), vmem(bias_table.shape[::-1], F32), dma((9,)),
             dma((5 + steps,)), dma((5 + steps,)),
             dma((steps + 2,)), dma((steps + 2,)), dma((2,)),
             dma((rows_n,)), dma((rows_n,)), dma((rows_n,)), dma((rows_n,)),
             dma((rows_n,)), dma((rows_n,)),
         ],
         compiler_params=pltpu.CompilerParams(
-            collective_id=0, has_side_effects=True, vmem_limit_bytes=48 * 1024 * 1024
+            collective_id=0, has_side_effects=True, vmem_limit_bytes=61 * 1024 * 1024
         ),
     )(
-        jnp.concatenate([tokens, grad_out], -1), regions, ln_gain.reshape(1, C), ln_offset.reshape(1, C), qkv_weight,
+        jnp.transpose(tokens, (2, 0, 1)), jnp.transpose(grad_out, (2, 0, 1)), regions, ln_gain.reshape(1, C), ln_offset.reshape(1, C), qkv_weight,
         qkv_bias, proj_weight, bias_table.T,
     )
-    shapes = [jax.ShapeDtypeStruct(x.shape, x.dtype) for x in outs]
-    shapes[2] = jax.ShapeDtypeStruct((3 * C,), F32)
     anywhere = pl.BlockSpec(memory_space=pl.ANY)
     d_tokens, d_qkvw, d_qkvb, d_projw, d_table, d_gain, d_offset = pl.pallas_call(
         finish,
-        out_shape=shapes,
-        in_specs=[whole] * 7,
+        out_shape=[jax.ShapeDtypeStruct(x.shape, x.dtype) for x in outs],
+        in_specs=[anywhere] * 7,
         out_specs=[anywhere] * 7,
-        scratch_shapes=[vmem((3 * C,), F32), dma((7,))],
-        compiler_params=pltpu.CompilerParams(vmem_limit_bytes=1024 * 1024),
+        scratch_shapes=[vmem(x.shape, x.dtype) for x in outs] + [dma((2, 7))],
+        compiler_params=pltpu.CompilerParams(vmem_limit_bytes=61 * 1024 * 1024),
     )(*outs)
     return (
         jnp.transpose(d_tokens, (1, 2, 0)),

time: 40.6 us -> 39.2 us (0.966)
  local copies, waits for them, and re-layouts: 2.25 us -> 0 us
  Pallas kernels: 37.2 us -> 38.4 us
    unnamed x18 -> x0, local copies, waits for them, and re-layouts: 2.25 us -> none
    pallas_call x1, Pallas kernels: 1.03 us -> 2.1 us  [on_device(): pl.pallas_call(finish, out_shape=[jax.ShapeDtypeStruct(x.shape, x.dtype)...]
where the time goes in v5:
time: 39.2 us; the launch traced here: 39 us
  Pallas kernels  38.4 us (98%)
  between operations  0.64 us (2%)
    pallas_call x1, Pallas kernels, on_device(): pl.pallas_call(functools.partial(body, rows_n, cols_n, rows_total, total_...  36.3 us
    pallas_call x1, Pallas kernels, on_device(): pl.pallas_call(finish, out_shape=[jax.ShapeDtypeStruct(x.shape, x.dtype)...  2.1 us

profile of v5, /device:TPU:0, one launch (start us, length us, event | category | flops | bytes accessed | tf_op | source)
XLA Modules:
  0.0 39.0 jit_solution(11759670845204503513)
XLA Ops:
  0.6 36.3 %shard_map.144 = (bf16[180,8,128]{2,1,0:T(8,128)(2,1)}, f32[180,540]{1,0:T(8,128)}, f32[540]{0:T(1024)}, f32[180,180]{1,0:T(8,128)}, f32[6,225]{1,0:T(8,128)}, /*index=5*/f32[1,180]{1,0:T(1,128)}, f32[1,180]{1,0:T(1,128)}) custom-call(bf16[180,8,128]{2,1,0:T(8,128)(2,1)} %bitcast.9, bf16[180,8,128]{2,1,0:T(8,128)(2,1)} %bitcast.10, s32[8,128]{1,0:T(8,128)} %reg_in.1, ...), custom_call_target="tpu_custom_call" | custom-call | tf_op jit(solution)/shard_map/pallas_call | solution.py:525
  36.9 2.1 %shard_map.145 = (bf16[180,8,128]{2,1,0:T(8,128)(2,1)}, f32[180,540]{1,0:T(8,128)}, f32[540]{0:T(1024)}, f32[180,180]{1,0:T(8,128)}, f32[6,225]{1,0:T(8,128)}, /*index=5*/f32[1,180]{1,0:T(1,128)}, f32[1,180]{1,0:T(1,128)}) custom-call(bf16[180,8,128]{2,1,0:T(8,128)(2,1)} %get-tuple-element.21.refs_0_, f32[180,540]{1,0:T(8,128)} %get-tuple-element.22.refs_1_, ...), custom_call_target="tpu_custom_call" | custom-call | tf_op jit(solution)/shard_map/pallas_call | solution.py:594

commit v6 on v5

--- a/solution.py
+++ b/solution.py
@@ -89,7 +89,7 @@
 
 
 def window_steps(wins):
-    return [(w, 4) for w in range(wins - 4, 0, -4)] + [(2, 2), (0, 2)]
+    return [(w, 4) for w in range(wins - 4, -1, -4)]
 
 
 def body(
@@ -171,8 +171,8 @@
     corner_on = halo(4, both_b.at[0:SHIFT, 0:EDGE], both_d, row, other)
     chunks = []
     for b, (w0, n) in enumerate(plan):
-        cols = slice(w0 * WIN, (w0 + n) * WIN)
-        chunks.append([halo(5 + b, both.at[SHIFT:WIN, cols], both_b.at[0:SHIFT, cols], down, col)] if w0 else [])
+        cols = slice(max(w0 * WIN, EDGE), (w0 + n) * WIN)
+        chunks.append([halo(5 + b, both.at[SHIFT:WIN, cols], both_b.at[0:SHIFT, cols], down, col)])
     ahead = 9
     small = 6 * BLOCK
     for copy in labels + [corner] + sum(chunks[:ahead], []):

time: 39.2 us -> 38.2 us (0.974)
  Pallas kernels: 38.4 us -> 37.4 us
    pallas_call x1, Pallas kernels: 36.3 us -> 35.3 us  [on_device(): pl.pallas_call(functools.partial(body, rows_n, cols_n, rows_total, total_...]
where the time goes in v6:
time: 38.2 us; the launch traced here: 38 us
  Pallas kernels  37.4 us (98%)
  between operations  0.64 us (2%)
    pallas_call x1, Pallas kernels, on_device(): pl.pallas_call(functools.partial(body, rows_n, cols_n, rows_total, total_...  35.3 us
    pallas_call x1, Pallas kernels, on_device(): pl.pallas_call(finish, out_shape=[jax.ShapeDtypeStruct(x.shape, x.dtype)...  2.1 us

profile of v6, /device:TPU:0, one launch (start us, length us, event | category | flops | bytes accessed | tf_op | source)
XLA Modules:
  0.0 38.0 jit_solution(12341274968890047537)
XLA Ops:
  0.6 35.3 %shard_map.144 = (bf16[180,8,128]{2,1,0:T(8,128)(2,1)}, f32[180,540]{1,0:T(8,128)}, f32[540]{0:T(1024)}, f32[180,180]{1,0:T(8,128)}, f32[6,225]{1,0:T(8,128)}, /*index=5*/f32[1,180]{1,0:T(1,128)}, f32[1,180]{1,0:T(1,128)}) custom-call(bf16[180,8,128]{2,1,0:T(8,128)(2,1)} %bitcast.9, bf16[180,8,128]{2,1,0:T(8,128)(2,1)} %bitcast.10, s32[8,128]{1,0:T(8,128)} %reg_in.1, ...), custom_call_target="tpu_custom_call" | custom-call | tf_op jit(solution)/shard_map/pallas_call | solution.py:525
  35.9 2.1 %shard_map.145 = (bf16[180,8,128]{2,1,0:T(8,128)(2,1)}, f32[180,540]{1,0:T(8,128)}, f32[540]{0:T(1024)}, f32[180,180]{1,0:T(8,128)}, f32[6,225]{1,0:T(8,128)}, /*index=5*/f32[1,180]{1,0:T(1,128)}, f32[1,180]{1,0:T(1,128)}) custom-call(bf16[180,8,128]{2,1,0:T(8,128)(2,1)} %get-tuple-element.21.refs_0_, f32[180,540]{1,0:T(8,128)} %get-tuple-element.22.refs_1_, ...), custom_call_target="tpu_custom_call" | custom-call | tf_op jit(solution)/shard_map/pallas_call | solution.py:594

commit v7 on v6

--- a/solution.py
+++ b/solution.py
@@ -173,7 +173,7 @@
     for b, (w0, n) in enumerate(plan):
         cols = slice(max(w0 * WIN, EDGE), (w0 + n) * WIN)
         chunks.append([halo(5 + b, both.at[SHIFT:WIN, cols], both_b.at[0:SHIFT, cols], down, col)])
-    ahead = 9
+    ahead = 3
     small = 6 * BLOCK
     for copy in labels + [corner] + sum(chunks[:ahead], []):
         copy.start()

time: 38.2 us -> 38.2 us (level)
  no operation moved by 1% of the time
where the time goes in v7:
time: 38.2 us; the launch traced here: 38 us
  Pallas kernels  37.4 us (98%)
  between operations  0.64 us (2%)
    pallas_call x1, Pallas kernels, on_device(): pl.pallas_call(functools.partial(body, rows_n, cols_n, rows_total, total_...  35.3 us
    pallas_call x1, Pallas kernels, on_device(): pl.pallas_call(finish, out_shape=[jax.ShapeDtypeStruct(x.shape, x.dtype)...  2.1 us

profile of v7, /device:TPU:0, one launch (start us, length us, event | category | flops | bytes accessed | tf_op | source)
XLA Modules:
  0.0 38.0 jit_solution(12586568013653969116)
XLA Ops:
  0.6 35.3 %shard_map.144 = (bf16[180,8,128]{2,1,0:T(8,128)(2,1)}, f32[180,540]{1,0:T(8,128)}, f32[540]{0:T(1024)}, f32[180,180]{1,0:T(8,128)}, f32[6,225]{1,0:T(8,128)}, /*index=5*/f32[1,180]{1,0:T(1,128)}, f32[1,180]{1,0:T(1,128)}) custom-call(bf16[180,8,128]{2,1,0:T(8,128)(2,1)} %bitcast.9, bf16[180,8,128]{2,1,0:T(8,128)(2,1)} %bitcast.10, s32[8,128]{1,0:T(8,128)} %reg_in.1, ...), custom_call_target="tpu_custom_call" | custom-call | tf_op jit(solution)/shard_map/pallas_call | solution.py:525
  35.9 2.1 %shard_map.145 = (bf16[180,8,128]{2,1,0:T(8,128)(2,1)}, f32[180,540]{1,0:T(8,128)}, f32[540]{0:T(1024)}, f32[180,180]{1,0:T(8,128)}, f32[6,225]{1,0:T(8,128)}, /*index=5*/f32[1,180]{1,0:T(1,128)}, f32[1,180]{1,0:T(1,128)}) custom-call(bf16[180,8,128]{2,1,0:T(8,128)(2,1)} %get-tuple-element.21.refs_0_, f32[180,540]{1,0:T(8,128)} %get-tuple-element.22.refs_1_, ...), custom_call_target="tpu_custom_call" | custom-call | tf_op jit(solution)/shard_map/pallas_call | solution.py:594
